TPU v7x, 512 devices: a whole 4x4x16 slice. The times are simulated.
512 devices in a mesh: segment: 32 (over y, x, core), tensor: 16 (over z).
Axes of the slice: x: 4, y: 4, z: 16, core: 2. Of those that a mesh axis runs over, the one named last changes fastest.
Arguments:
- h_init: bfloat16 [256, 4096], P('segment', 'tensor'), may hold values from -6 to 6
- y_init: bfloat16 [256, 4096], P('segment', 'tensor'), may hold values from -6 to 6
- norm_gain: bfloat16 [32, 4096], P('segment'), may hold values from 0.099609375 to 1.8984375
- w_query: bfloat16 [32, 4096, 4096], P('segment', None, 'tensor'), may hold values from -0.09375 to 0.09375
- w_kv: bfloat16 [32, 4096, 1024], P('segment', 'tensor'), may hold values from -0.09375 to 0.09375
- w_out: bfloat16 [32, 4096, 4096], P('segment', 'tensor'), may hold values from -0.09375 to 0.09375
- cache: bfloat16 [32, 16, 224, 1024], P('segment', None, 'tensor'), may hold values from -400 to 400
- lengths: int32 [256], replicated, may hold values from 1 to 224, as said below
Outputs:
- h_final: bfloat16 [256, 4096], P('segment', 'tensor')
- y_final: bfloat16 [256, 4096], P('segment', 'tensor')
Inputs may be any that keep to these rules, and one draw needn't show every extreme that they name: `lengths`: some row has exactly 224 cached positions.
All inputs are finite; a program needn't handle non-finite values.
Results may differ from a plain program's by a relative error of at most 0.025.
The roundings to bfloat16 on the way count: a program that leaves them out, or rounds other values in their place, can miss the bound.
Values may be sent and summed in bfloat16 or wider, within the bound.
A program may use at most 64 MiB of HBM per device.

v0:
```python
import jax
import jax.numpy as jnp
from jax import lax
from jax.sharding import PartitionSpec as P

HEADS = 32
KVH = 4
HD = 128
TICKS = 2


theta_base = 500000.0
eps_norm = 1e-05
masked_score = -1e30


def merged(x, axis, combine):
    everything = jax.tree.map(lambda part: lax.all_gather(part, axis), x)
    leading = jax.tree.map(lambda part: part[0], everything)

    def lap(k, so_far):
        return combine(so_far, jax.tree.map(lambda part: part[k], everything))

    return lax.fori_loop(1, lax.axis_size(axis), lap, leading)


def shifted(value, axis, steps):
    count = lax.axis_size(axis)
    leading, last = (max(0, -steps), min(count, count - steps))
    return lax.ppermute(value, axis, [(source, source + steps) for source in range(leading, last)])


def rotate(values, positions):
    row_count = values.shape[0]
    head_count = values.shape[1] // HD
    half_size = HD // 2
    freqs = jnp.exp(-jnp.log(theta_base) * (2.0 * jnp.arange(half_size, dtype=jnp.float32) / HD))
    angles = positions.astype(jnp.float32)[:, None] * freqs[None, :]
    cosine = jnp.cos(angles)[:, None, :]
    sine = jnp.sin(angles)[:, None, :]
    shaped = values.reshape(row_count, head_count, HD)
    first_half = shaped[..., :half_size]
    second_half = shaped[..., half_size:]
    turned = jnp.concatenate(
        [first_half * cosine - second_half * sine, second_half * cosine + first_half * sine],
        axis=-1,
    )
    return turned.reshape(row_count, head_count * HD)


def combine_parts(first, second):
    peak = jnp.maximum(first[0], second[0])
    first_scale = jnp.exp(first[0] - peak)
    second_scale = jnp.exp(second[0] - peak)
    return (
        peak,
        first[1] * first_scale + second[1] * second_scale,
        first[2] * first_scale[..., None] + second[2] * second_scale[..., None],
    )


def sum_fresh(kv_terms):
    return lax.psum(kv_terms.astype(jnp.bfloat16), "tensor").astype(jnp.float32)


def local(h_init, y_init, norm_gain, w_query, w_kv, w_out, cache, lengths):
    tensor_count = lax.axis_size("tensor")
    tensor_rank = lax.axis_index("tensor")
    segment_rank = lax.axis_index("segment")
    micro_rows = h_init.shape[0]
    query_weight = w_query[0]
    kv_weight = w_kv[0]
    out_weight = w_out[0]
    gain_row = norm_gain[0].astype(jnp.float32)
    resident_cache = cache[0]
    heads_local = query_weight.shape[1] // HD
    slice_width = kv_weight.shape[0]
    model_width = out_weight.shape[1]
    width_share = model_width // tensor_count
    span_local = resident_cache.shape[1]
    key_width = KVH * HD
    group_size = HEADS // KVH
    softmax_scale = HD ** (-0.5)
    state, waiting = (
        lax.all_gather(h_init, "tensor", axis=1, tiled=True),
        lax.all_gather(y_init, "tensor", axis=1, tiled=True),
    )
    positions = tensor_rank * span_local + jnp.arange(span_local, dtype=jnp.int32)
    final_state = h_init
    block_share = h_init
    for step_index in range(TICKS):
        final_tick_index = step_index + 1 == TICKS
        batch_index = segment_rank - step_index
        picked = lax.dynamic_slice_in_dim(
            lengths, jnp.maximum(batch_index, 0) * micro_rows, micro_rows, 0
        )
        seen = jnp.where(batch_index >= 0, picked, 0)
        widened = state.astype(jnp.float32)
        normed = (
            widened
            * lax.rsqrt(jnp.mean(widened * widened, axis=-1, keepdims=True) + eps_norm)
            * gain_row
        ).astype(jnp.bfloat16)
        queries = rotate(
            jnp.dot(normed, query_weight, preferred_element_type=jnp.float32), seen
        ).astype(jnp.bfloat16)
        kv_terms = jnp.dot(
            lax.dynamic_slice_in_dim(normed, tensor_rank * slice_width, slice_width, 1),
            kv_weight,
            preferred_element_type=jnp.float32,
        )
        fresh = sum_fresh(kv_terms)
        fresh = jnp.concatenate(
            [rotate(fresh[:, :key_width], seen), fresh[:, key_width:]], axis=1
        ).astype(jnp.bfloat16)
        every_query = lax.all_gather(queries, "tensor", axis=1, tiled=True)
        rows_now = lax.slice_in_dim(
            resident_cache, step_index * micro_rows, (step_index + 1) * micro_rows, axis=0
        )
        query_head_rows = every_query.astype(jnp.float32).reshape(micro_rows, KVH, group_size, HD)
        cached_keys = (
            rows_now[..., :key_width].astype(jnp.float32).reshape(micro_rows, span_local, KVH, HD)
        )
        cached_values = (
            rows_now[..., key_width:].astype(jnp.float32).reshape(micro_rows, span_local, KVH, HD)
        )
        valid = positions[None, :] < seen[:, None]
        scores = jnp.einsum("bkgd,bpkd->bkgp", query_head_rows, cached_keys) * softmax_scale
        scores = jnp.where(valid[:, None, None, :], scores, masked_score)
        peak = jnp.max(scores, axis=-1)
        weights = jnp.where(valid[:, None, None, :], jnp.exp(scores - peak[..., None]), 0.0)
        weight_sum = jnp.sum(weights, axis=-1).reshape(micro_rows, HEADS)
        mixed = jnp.einsum("bkgp,bpkd->bkgd", weights, cached_values).reshape(micro_rows, HEADS, HD)
        peak = peak.reshape(micro_rows, HEADS)
        peak, weight_sum, mixed = merged((peak, weight_sum, mixed), "tensor", combine_parts)
        peak = lax.dynamic_slice_in_dim(peak, tensor_rank * heads_local, heads_local, 1)
        weight_sum = lax.dynamic_slice_in_dim(weight_sum, tensor_rank * heads_local, heads_local, 1)
        mixed = lax.dynamic_slice_in_dim(mixed, tensor_rank * heads_local, heads_local, 1)
        own_queries = queries.astype(jnp.float32).reshape(micro_rows, heads_local, HD)
        incoming_keys = jnp.repeat(
            fresh[:, :key_width].astype(jnp.float32).reshape(micro_rows, KVH, HD),
            group_size,
            axis=1,
        )
        incoming_values = jnp.repeat(
            fresh[:, key_width:].astype(jnp.float32).reshape(micro_rows, KVH, HD),
            group_size,
            axis=1,
        )
        own_keys = lax.dynamic_slice_in_dim(
            incoming_keys, tensor_rank * heads_local, heads_local, 1
        )
        own_values = lax.dynamic_slice_in_dim(
            incoming_values, tensor_rank * heads_local, heads_local, 1
        )
        self_token_score = jnp.sum(own_queries * own_keys, axis=-1) * softmax_scale
        highest = jnp.maximum(peak, self_token_score)
        old_scale = jnp.exp(peak - highest)
        own_weight = jnp.exp(self_token_score - highest)
        denominator = weight_sum * old_scale + own_weight
        attended_context = (
            mixed * old_scale[..., None] + own_weight[..., None] * own_values
        ) / denominator[..., None]
        attended_context = attended_context.reshape(micro_rows, heads_local * HD).astype(
            jnp.bfloat16
        )
        block_terms = jnp.dot(attended_context, out_weight, preferred_element_type=jnp.float32)
        advanced = (widened + waiting.astype(jnp.float32)).astype(jnp.bfloat16)
        block_out = lax.psum(block_terms.astype(jnp.bfloat16), "tensor")
        if final_tick_index:
            block_share = lax.dynamic_slice_in_dim(
                block_out, tensor_rank * width_share, width_share, 1
            )
            final_state = lax.dynamic_slice_in_dim(
                advanced, tensor_rank * width_share, width_share, 1
            )
        else:
            state, waiting = shifted((advanced, block_out), "segment", 1)
    return (final_state, block_share)


def solution(mesh):
    return jax.shard_map(
        local,
        mesh=mesh,
        in_specs=(
            P("segment", "tensor"),
            P("segment", "tensor"),
            P("segment", None),
            P("segment", None, "tensor"),
            P("segment", "tensor", None),
            P("segment", "tensor", None),
            P("segment", None, "tensor", None),
            P(),
        ),
        out_specs=(P("segment", "tensor"), P("segment", "tensor")),
        check_vma=False,
    )
```

profile of v0, /device:TPU:24, one launch (start us, length us, event | category | flops | bytes accessed | tf_op | source)
XLA Modules:
  0.0 543.8 jit_solution(12353588193187809333)
XLA Ops:
  7.2 36.1 %all_gather.30 = bf16[8,4096]{1,0:T(8,128)(2,1)S(1)} all-gather(bf16[8,256]{1,0:T(8,128)(2,1)} %param.12), channel_id=1, replica_groups=mesh['segment'=32,'tensor'=16] {'tensor'}, dimensions={1}, use_global_device_ids=true | all-gather | bytes 69632 | tf_op jit(solution)/shard_map/all_gather | solution.py:85
  44.3 26.6 %all_gather.31 = bf16[8,4096]{1,0:T(8,128)(2,1)S(1)} all-gather(bf16[8,256]{1,0:T(8,128)(2,1)} %param.13), channel_id=1, replica_groups=mesh['segment'=32,'tensor'=16] {'tensor'}, dimensions={1}, use_global_device_ids=true | all-gather | bytes 69632 | tf_op jit(solution)/shard_map/all_gather | solution.py:86
  71.5 1.9 collective-permute-start
  73.9 4.2 copy.40
  78.7 2.2 fusion.28
  83.1 2.2 fusion.26
  85.5 54.5 %all-reduce = (bf16[8,1024]{1,0:T(8,128)(2,1)S(1)}, bf16[8,1024]{1,0:T(8,128)(2,1)S(1)}) all-reduce(bf16[8,1024]{1,0:T(8,128)(2,1)S(1)} %convolution_convert_fusion.3, bf16[8,1024]{1,0:T(8,128)(2,1)S(1)} %convolution_convert_fusion.2), channel_id=1, replica_groups=mesh['segment'=32,'tensor'=16] {'tensor'}, use_global_device_ids=true, to_apply=%region_5.6 | all-reduce | flops 16384 | bytes 65536 | tf_op jit(solution)/shard_map/psum | solution.py:63
  140.5 26.2 %all_gather.36 = bf16[8,4096]{1,0:T(8,128)(2,1)S(1)} all-gather(bf16[8,256]{1,0:T(8,128)(2,1)S(1)} %bitcast.150), channel_id=1, replica_groups=mesh['segment'=32,'tensor'=16] {'tensor'}, dimensions={1}, use_global_device_ids=true | all-gather | bytes 69632 | tf_op jit(solution)/shard_map/all_gather | solution.py:116
  168.7 28.3 %all_gather.32 = bf16[8,4096]{1,0:T(8,128)(2,1)S(1)} all-gather(bf16[8,256]{1,0:T(8,128)(2,1)S(1)} %bitcast.151), channel_id=1, replica_groups=mesh['segment'=32,'tensor'=16] {'tensor'}, dimensions={1}, use_global_device_ids=true | all-gather | bytes 69632 | tf_op jit(solution)/shard_map/all_gather | solution.py:116
  197.7 26.4 %all_gather.38 = f32[16,8,32]{2,1,0:T(8,128)S(1)} all-gather(f32[1,8,32]{2,1,0:T(8,128)S(1)} %all_gather_reshape.22), channel_id=1, replica_groups=mesh['segment'=32,'tensor'=16] {'tensor'}, dimensions={0}, use_global_device_ids=true | all-gather | bytes 17408 | tf_op jit(solution)/shard_map/all_gather | solution.py:18
  224.0 28.2 %all_gather.37 = f32[16,8,32]{2,1,0:T(8,128)S(1)} all-gather(f32[1,8,32]{2,1,0:T(8,128)S(1)} %all_gather_reshape.21), channel_id=1, replica_groups=mesh['segment'=32,'tensor'=16] {'tensor'}, dimensions={0}, use_global_device_ids=true | all-gather | bytes 17408 | tf_op jit(solution)/shard_map/all_gather | solution.py:18
  252.2 26.3 %all_gather.34 = f32[16,8,32]{2,1,0:T(8,128)S(1)} all-gather(f32[1,8,32]{2,1,0:T(8,128)S(1)} %all_gather_reshape.19), channel_id=1, replica_groups=mesh['segment'=32,'tensor'=16] {'tensor'}, dimensions={0}, use_global_device_ids=true | all-gather | bytes 17408 | tf_op jit(solution)/shard_map/all_gather | solution.py:18
  278.5 28.2 %all_gather.33 = f32[16,8,32]{2,1,0:T(8,128)S(1)} all-gather(f32[1,8,32]{2,1,0:T(8,128)S(1)} %all_gather_reshape.18), channel_id=1, replica_groups=mesh['segment'=32,'tensor'=16] {'tensor'}, dimensions={0}, use_global_device_ids=true | all-gather | bytes 17408 | tf_op jit(solution)/shard_map/all_gather | solution.py:18
  308.7 16.8 %while.39 = (s32[]{:T(128)}, f32[8,32]{1,0:T(8,128)S(1)}, f32[8,32]{1,0:T(8,128)S(1)}, f32[8,32,128]{2,1,0:T(8,128)S(1)}, f32[16,8,32]{2,1,0:T(8,128)S(1)}, /*in...) while((s32[]{:T(128)}, f32[8,32]{1,0:T(8,128)S(1)}, ...), condition=%wide.region_12.13_spmd, body=%wide.region_11.12_spmd.sunk | while | flops 99845 | bytes 403607 | solution.py:24
  308.7 1.1 fusion.82
  309.8 1.1 fusion.82
  312.1 1.1 fusion.82
  314.3 1.1 fusion.82
  325.9 50.8 %all-gather.3.cloned.1.call-done = f32[16,8,32,128]{3,2,1,0:T(8,128)} async-done(((f32[1,8,32,128]{3,2,1,0:T(8,128)}), f32[16,8,32,128]{3,2,1,0:T(8,128)}) %all-gather.3.cloned.1.call-update) | async-done | bytes 2097168 | tf_op jit(solution)/shard_map/all_gather | solution.py:18
  377.6 16.8 %while.38 = (s32[]{:T(128)}, f32[8,32]{1,0:T(8,128)S(1)}, f32[8,32]{1,0:T(8,128)S(1)}, f32[8,32,128]{2,1,0:T(8,128)S(1)}, f32[16,8,32]{2,1,0:T(8,128)S(1)}, /*in...) while((s32[]{:T(128)}, f32[8,32]{1,0:T(8,128)S(1)}, ...), condition=%wide.region_4.5_spmd, body=%wide.region_3.4_spmd.sunk | while | flops 99845 | bytes 403607 | solution.py:24
  397.1 131.7 %all-reduce.4.cloned.1.call-done = (bf16[8,4096]{1,0:T(8,128)(2,1)}, bf16[8,4096]{1,0:T(8,128)(2,1)}) async-done(((bf16[8,4096]{1,0:T(8,128)(2,1)}, bf16[8,4096]{1,0:T(8,128)(2,1)}), (bf16[8,4096]{1,0:T(8,128)(2,1)}, bf16[8,4096]{1,0:T(8,128)(2,1)})) %all-reduce.4.cloned.1.call-update) | async-done | bytes 131088 | tf_op jit(solution)/shard_map/psum | solution.py:169
  528.8 1.9 collective-permute-start.1
  530.7 1.3 constant_dynamic-slice_fusion.4
  532.0 4.7 collective-permute-done.1
  (141 shorter events, 42.9 us)
Async XLA Ops:
  7.2 387.8 %copy-start = (bf16[1,256,4096]{2,1,0:T(8,128)(2,1)S(1)}, bf16[1,256,4096]{2,1,0:T(8,128)(2,1)}, u32[]{:S(2)}) copy-start(bf16[1,256,4096]{2,1,0:T(8,128)(2,1)} %param.17) | copy-start | bytes 6291460
  7.2 300.6 %all-gather.5.cloned.1.call-start = ((), (), s32[]{:S(2)}) async-start(), calls=%async_computation.1 | async-start | bytes 2228224 | tf_op jit(solution)/shard_map/all_gather | solution.py:18
  44.2 27.2 %copy-start.3 = (f32[1,4096]{1,0:T(1,128)}, f32[1,4096]{1,0:T(1,128)S(1)}, u32[]{:S(2)}) copy-start(f32[1,4096]{1,0:T(1,128)S(1)} %mul.516) | copy-start | bytes 49156
  71.5 11.4 %collective-permute-start = (bf16[8,4096]{1,0:T(8,128)(2,1)}, bf16[8,4096]{1,0:T(8,128)(2,1)S(1)}, u32[]{:S(2)}, u32[]{:S(2)}) collective-permute-start(bf16[8,4096]{1,0:T(8,128)(2,1)} %get-tuple-element.425), channel_id=1, source_target_pairs={{0,16},{16,32},{32,48},{48,64},{64,80},{80,96},{96,112},{112,128},... | collective-permute-start | bytes 196616 | tf_op jit(solution)/shard_map/ppermute | solution.py:30
  73.9 4.7 copy-start.2
  78.1 2.8 copy-start.1
  78.6 4.1 copy-start.5
  78.7 4.3 copy-start.4
  167.9 208.8 %all-gather.3.cloned.1.call-start = ((), (), s32[]{:S(2)}) async-start(), calls=%async_computation | async-start | bytes 2228224 | tf_op jit(solution)/shard_map/all_gather | solution.py:18
  307.7 221.1 %all-reduce.4.cloned.1.call-start = ((), (), s32[]{:S(2)}) async-start(), calls=%async_computation.2 | async-start | bytes 262144 | tf_op jit(solution)/shard_map/psum | solution.py:169
  528.8 7.9 %collective-permute-start.1 = (bf16[8,4096]{1,0:T(8,128)(2,1)}, bf16[8,4096]{1,0:T(8,128)(2,1)S(1)}, u32[]{:S(2)}, u32[]{:S(2)}) collective-permute-start(bf16[8,4096]{1,0:T(8,128)(2,1)} %get-tuple-element.394), channel_id=1, source_target_pairs={{0,16},{16,32},{32,48},{48,64},{64,80},{80,96},{96,112},{112,128},... | collective-permute-start | bytes 196616 | tf_op jit(solution)/shard_map/ppermute | solution.py:30
Sparse Core Ops, SparseCore 0:
  168.0 69.7 all-gather.4
  307.8 68.8 all-gather.2
  397.2 131.5 all-reduce.3
where the time goes:
time: 545 us; the launch traced here: 544 us
  blocking collectives  281 us (52%)
  waiting for transfers between devices  187 us (34%)
  other arithmetic  39.2 us (7%)
  between operations  14 us (3%)
  matrix products  9.2 us (2%)
  local copies, waits for them, and re-layouts  8.54 us (2%)
    psum x1, waiting for transfers between devices, local(): block_out = lax.psum(block_terms.astype(jnp.bfloat16), 'tensor')  132 us
    all_gather x4, blocking collectives, merged(): everything = jax.tree.map(lambda part: lax.all_gather(part, axis), x)  109 us
    all_gather x2, blocking collectives, local(): every_query = lax.all_gather(queries, 'tensor', axis=1, tiled=True)  54.5 us
    psum x1, blocking collectives, sum_fresh(): return lax.psum(kv_terms.astype(jnp.bfloat16), 'tensor').astype(jnp.float32)  54.5 us
    all_gather x2, waiting for transfers between devices, merged(): everything = jax.tree.map(lambda part: lax.all_gather(part, axis), x)  50.8 us
    all_gather x1, blocking collectives, local(): lax.all_gather(h_init, 'tensor', axis=1, tiled=True)  36.1 us
    add x30, other arithmetic, combine_parts(): first[2] * first_scale[..., None] + second[2] * second_scale[..., None]  32.2 us
    all_gather x1, blocking collectives, local(): lax.all_gather(y_init, 'tensor', axis=1, tiled=True)  26.6 us
  transfers between devices with their start and end apart: 5, of which 3 were waited for; matrix products, arithmetic and copies ran while one was open for 6% of the time, Pallas kernels for 0%

commit v1 on v0

v1 whole, which is shorter than its diff:
```python
import functools
import math

import jax
import jax.numpy as jnp
from jax import lax
from jax.experimental import pallas as pl
from jax.experimental.pallas import tpu as pltpu
from jax.sharding import PartitionSpec as P

HEADS = 32
KVH = 4
HD = 128
TICKS = 2
MB = 8
ROWS2 = TICKS * MB
THETA = 500000.0
EPS = 1e-05
MASKED = -1e30
BIG = 1 << 30
MESH = pl.DeviceIdType.MESH
F32 = jnp.float32
BF16 = jnp.bfloat16


def far_first(i, me, n):
    d = n // 2 - (i + 1) // 2
    off = jnp.where(lax.rem(i, 2) == 1, d, n - d)
    return lax.rem(me + off, n)


def drain(ref, sem):
    pltpu.make_async_copy(ref, ref, sem).wait()


def stack_halves(v):
    return jnp.concatenate([v[:, :HD], v[:, HD:]], axis=0)


def unstack(v):
    return jnp.concatenate([v[:MB], v[MB:]], axis=1)


def kernel(
    n, n_seg, h_hbm, y_hbm, gain_hbm, wq_hbm, wkv_hbm, wo_hbm, cache_hbm, len_ref,
    hfin_ref, yfin_ref,
    h_in, y_in, gain, wq, wkv, wo, cache,
    hsrc, asrc, hbuf, abuf, nbuf, cosb, sinb,
    qsrc, qbuf, kvsrc, kvbuf, kbuf, vbuf, qt, ot,
    osrc, obuf, ssrc, sbuf,
    d0src, d1src, d0buf, d1buf,
    load_sem, send_sem, recv_sem,
):
    me = lax.axis_index("tensor")
    seg = lax.axis_index("segment")
    first = seg == 0
    last = seg == n_seg - 1
    span = cache_hbm.shape[2]

    barrier = pltpu.get_barrier_semaphore()

    def tell(i, carry):
        pl.semaphore_signal(
            barrier, 1, device_id={"tensor": far_first(i, me, n)}, device_id_type=MESH
        )
        return carry

    lax.fori_loop(0, n - 1, tell, 0)

    @pl.when(seg > 0)
    def _():
        def tell_back(i, carry):
            pl.semaphore_signal(
                barrier, 1, device_id={"segment": seg - 1, "tensor": i}, device_id_type=MESH
            )
            return carry

        lax.fori_loop(0, n, tell_back, 0)

    loads = [
        pltpu.make_async_copy(src, dst, load_sem.at[k])
        for k, (src, dst) in enumerate(
            [
                (h_hbm, h_in), (y_hbm, y_in), (gain_hbm, gain), (cache_hbm, cache),
                (wkv_hbm, wkv), (wq_hbm, wq), (wo_hbm, wo),
            ]
        )
    ]
    for load in loads:
        load.start()
    loads[0].wait()
    loads[1].wait()

    h32 = h_in[...].astype(F32)
    a32 = (h32 + y_in[...].astype(F32)).astype(BF16).astype(F32)
    h_block = stack_halves(h32).astype(BF16)
    hsrc[...] = h_block
    asrc[...] = stack_halves(a32).astype(BF16)
    hbuf[me] = h_block

    row16 = lax.broadcasted_iota(jnp.int32, (ROWS2, HD), 0)
    lane16 = lax.broadcasted_iota(jnp.int32, (ROWS2, HD), 1)
    base1 = jnp.maximum(seg - 1, 0) * MB
    seen = [len_ref[seg * MB + b] for b in range(MB)] + [
        jnp.where(first, 0, len_ref[base1 + b]) for b in range(MB)
    ]
    seen_rows = jnp.zeros((ROWS2, HD), jnp.int32)
    for b in range(ROWS2):
        seen_rows = jnp.where(row16 == b, seen[b], seen_rows)
    half_lane = jnp.where(lane16 < HD // 2, lane16, lane16 - HD // 2)
    freqs = jnp.exp(-math.log(THETA) * (2.0 * half_lane.astype(F32) / HD))
    angles = seen_rows.astype(F32) * freqs
    sines = jnp.sin(angles)
    cosb[...] = jnp.cos(angles)
    sinb[...] = jnp.where(lane16 < HD // 2, -sines, sines)

    pl.semaphore_wait(barrier, jnp.where(last, n - 1, 2 * n - 1))

    def send_state(i, carry):
        peer = far_first(i, me, n)
        pltpu.make_async_remote_copy(
            hsrc, hbuf.at[me], send_sem.at[0], recv_sem.at[0],
            device_id={"tensor": peer}, device_id_type=MESH,
        ).start()
        return carry

    def send_both(i, carry):
        peer = far_first(i, me, n)
        pltpu.make_async_remote_copy(
            asrc, abuf.at[me], send_sem.at[1], recv_sem.at[1],
            device_id={"segment": seg + 1, "tensor": peer}, device_id_type=MESH,
        ).start()
        return send_state(i, carry)

    @pl.when(seg < n_seg - 1)
    def _():
        lax.fori_loop(0, n - 1, send_both, 0)
        pltpu.make_async_remote_copy(
            asrc, abuf.at[me], send_sem.at[1], recv_sem.at[1],
            device_id={"segment": seg + 1, "tensor": me}, device_id_type=MESH,
        ).start()

    @pl.when(last)
    def _():
        lax.fori_loop(0, n - 1, send_state, 0)

    loads[3].wait()
    pad = jnp.zeros((16 - span, HD), F32)
    for b in range(ROWS2):
        rows = cache[0, b].astype(F32)
        for dst, start in ((kbuf, 0), (vbuf, KVH * HD)):
            dst[b] = jnp.concatenate(
                [
                    piece
                    for g in range(KVH)
                    for piece in (rows[:, start + g * HD : start + (g + 1) * HD], pad)
                ],
                axis=0,
            ).astype(BF16)
    loads[2].wait()

    @pl.when(first)
    def _():
        abuf[...] = jnp.zeros_like(abuf)
        d0buf[...] = jnp.zeros_like(d0buf)

    loads[4].wait()
    loads[5].wait()
    drain(hbuf.at[pl.ds(0, n - 1)], recv_sem.at[0])

    @pl.when(seg > 0)
    def _():
        drain(abuf, recv_sem.at[1])

    chunks = []
    for z in range(n):
        hz = hbuf[z].astype(F32)
        az = abuf[z].astype(F32)
        chunks.append(jnp.concatenate([hz[:MB], az[:MB]], axis=0))
        chunks.append(jnp.concatenate([hz[MB:], az[MB:]], axis=0))
    squares = [c * c for c in chunks]
    while len(squares) > 1:
        squares = [a + b for a, b in zip(squares[::2], squares[1::2])]
    mean = jnp.sum(squares[0], axis=-1, keepdims=True) / (n * 2 * HD)
    inv = lax.rsqrt(mean + EPS)
    normed = []
    for k, c in enumerate(chunks):
        g = gain[0:1, k * HD : (k + 1) * HD].astype(F32)
        normed.append((c * inv * g).astype(BF16))
    for z in range(n):
        nbuf[z] = jnp.concatenate(normed[2 * z : 2 * z + 2], axis=1)
    kv = jnp.dot(nbuf[me], wkv[0], preferred_element_type=F32)
    for c in range(2 * KVH):
        kvsrc[pl.ds(c, ROWS2, stride=2 * KVH), :] = kv[:, c * HD : (c + 1) * HD]
    q32 = jnp.dot(jnp.concatenate(normed, axis=1), wq[0], preferred_element_type=F32)
    cosine = cosb[...]
    sine = sinb[...]
    turned = []
    for i in range(2):
        v = q32[:, i * HD : (i + 1) * HD]
        turned.append(v * cosine + pltpu.roll(v, HD // 2, 1) * sine)
    q = jnp.concatenate(turned, axis=1).astype(BF16)
    qsrc[...] = q
    qbuf[me] = q
    kvbuf[me] = kvsrc[pl.ds(pl.multiple_of(me * 8, 8), 8), :]

    def send_query(i, carry):
        peer = far_first(i, me, n)
        pltpu.make_async_remote_copy(
            kvsrc.at[pl.ds(pl.multiple_of(peer * 8, 8), 8)], kvbuf.at[me],
            send_sem.at[3], recv_sem.at[3],
            device_id={"tensor": peer}, device_id_type=MESH,
        ).start()
        pltpu.make_async_remote_copy(
            qsrc, qbuf.at[me], send_sem.at[2], recv_sem.at[2],
            device_id={"tensor": peer}, device_id_type=MESH,
        ).start()
        return carry

    lax.fori_loop(0, n - 1, send_query, 0)

    jrow = lax.broadcasted_iota(jnp.int32, (HEADS, KVH * 16), 0)
    kcol = lax.broadcasted_iota(jnp.int32, (HEADS, KVH * 16), 1)
    same = lax.rem(jrow, 16) // 4 == kcol // 16
    slot = lax.rem(kcol, 16)
    place = jnp.where(same & (slot < span), me * span + slot, BIG)
    own_slot = same & (slot == span)
    lane32 = lax.broadcasted_iota(jnp.int32, (HEADS, HD), 1)

    drain(kvbuf.at[pl.ds(0, n - 1)], recv_sem.at[3])
    fresh = kvbuf[0]
    for z in range(1, n):
        fresh = fresh + kvbuf[z]
    fresh_k = fresh[:KVH]
    fresh_k = (
        fresh_k * cosb[pl.ds(me, 1), :]
        + pltpu.roll(fresh, HD // 2, 1)[:KVH] * sinb[pl.ds(me, 1), :]
    )
    fresh_v = fresh[KVH:]
    krow = lax.broadcasted_iota(jnp.int32, (KVH * 16, HD), 0)
    for dst, val in ((kbuf, fresh_k), (vbuf, fresh_v)):
        spread = jnp.concatenate(
            [jnp.broadcast_to(val[g : g + 1], (16, HD)) for g in range(KVH)], axis=0
        )
        dst[me] = jnp.where(lax.rem(krow, 16) == span, spread, dst[me].astype(F32)).astype(BF16)

    drain(qbuf.at[pl.ds(0, n - 1)], recv_sem.at[2])
    for r in range(n):
        v = qbuf[r].astype(F32)
        qt[0, pl.ds(r, ROWS2, stride=n), :] = v[:, :HD]
        qt[1, pl.ds(r, ROWS2, stride=n), :] = v[:, HD:]

    stats = jnp.zeros((HEADS, HD), F32)
    scale = HD ** (-0.5)
    for b in range(ROWS2):
        qb = jnp.concatenate(
            [qt[0, b * n : (b + 1) * n, :], qt[1, b * n : (b + 1) * n, :]], axis=0
        ).astype(BF16)
        s = (
            lax.dot_general(
                qb, kbuf[b], (((1,), (1,)), ((), ())), preferred_element_type=F32
            )
            * scale
        )
        own_place = jnp.where(me == b, -1, BIG)
        valid = jnp.where(own_slot, own_place, place) < seen[b]
        s = jnp.where(valid, s, MASKED)
        peak = jnp.max(s, axis=-1, keepdims=True)
        w = jnp.where(valid, jnp.exp(s - peak), 0.0)
        total = jnp.sum(w, axis=-1, keepdims=True)
        mixed = jnp.dot(w.astype(BF16), vbuf[b], preferred_element_type=F32)
        ot[0, b * n : (b + 1) * n, :] = mixed[:n]
        ot[1, b * n : (b + 1) * n, :] = mixed[n:]
        stats = jnp.where(lane32 == b, peak, stats)
        stats = jnp.where(lane32 == ROWS2 + b, total, stats)
    packed = jnp.where(lane32[:n] < 2 * ROWS2, stats[:n], pltpu.roll(stats[n:], 2 * ROWS2, 1))
    for r in range(n):
        ssrc[r] = packed[r : r + 1, :]
        osrc[r] = jnp.concatenate(
            [ot[0, pl.ds(r, ROWS2, stride=n), :], ot[1, pl.ds(r, ROWS2, stride=n), :]], axis=1
        ).astype(BF16)
    obuf[me] = osrc[me]
    sbuf[me] = ssrc[me]

    def send_partial(i, carry):
        peer = far_first(i, me, n)
        pltpu.make_async_remote_copy(
            ssrc.at[peer], sbuf.at[me], send_sem.at[5], recv_sem.at[5],
            device_id={"tensor": peer}, device_id_type=MESH,
        ).start()
        pltpu.make_async_remote_copy(
            osrc.at[peer], obuf.at[me], send_sem.at[4], recv_sem.at[4],
            device_id={"tensor": peer}, device_id_type=MESH,
        ).start()
        return carry

    lax.fori_loop(0, n - 1, send_partial, 0)
    drain(sbuf.at[pl.ds(0, n - 1)], recv_sem.at[5])
    by_row = jnp.transpose(jnp.concatenate([sbuf[r] for r in range(n)], axis=0))
    shares = []
    for i in range(2):
        peaks = by_row[i * 32 : i * 32 + 16]
        totals = by_row[i * 32 + 16 : i * 32 + 32]
        scales = jnp.exp(peaks - jnp.max(peaks, axis=-1, keepdims=True))
        shares.append(scales / jnp.sum(scales * totals, axis=-1, keepdims=True))
    loads[6].wait()
    drain(obuf.at[pl.ds(0, n - 1)], recv_sem.at[4])
    context = [jnp.zeros((ROWS2, HD), F32), jnp.zeros((ROWS2, HD), F32)]
    for r in range(n):
        v = obuf[r].astype(F32)
        for i in range(2):
            context[i] = context[i] + v[:, i * HD : (i + 1) * HD] * shares[i][:, r : r + 1]
    ctx = jnp.concatenate(context, axis=1).astype(BF16)

    out = jnp.dot(ctx, wo[0], preferred_element_type=F32)
    for c in range(n):
        block = out[:, c * 256 : (c + 1) * 256]
        d0src[c] = stack_halves(block[:MB]).astype(BF16)
        d1src[c] = stack_halves(block[MB:]).astype(BF16)
    d1buf[me] = d1src[me]

    def send_out(i, carry):
        peer = far_first(i, me, n)
        pltpu.make_async_remote_copy(
            d1src.at[peer], d1buf.at[me], send_sem.at[7], recv_sem.at[7],
            device_id={"tensor": peer}, device_id_type=MESH,
        ).start()
        return carry

    def send_outs(i, carry):
        peer = far_first(i, me, n)
        pltpu.make_async_remote_copy(
            d0src.at[peer], d0buf.at[me], send_sem.at[6], recv_sem.at[6],
            device_id={"segment": seg + 1, "tensor": peer}, device_id_type=MESH,
        ).start()
        return send_out(i, carry)

    @pl.when(seg < n_seg - 1)
    def _():
        lax.fori_loop(0, n - 1, send_outs, 0)
        pltpu.make_async_remote_copy(
            d0src.at[me], d0buf.at[me], send_sem.at[6], recv_sem.at[6],
            device_id={"segment": seg + 1, "tensor": me}, device_id_type=MESH,
        ).start()

    @pl.when(last)
    def _():
        lax.fori_loop(0, n - 1, send_out, 0)

    for _ in range(1):
        pltpu.make_async_copy(hbuf.at[pl.ds(0, n - 1)], hbuf.at[pl.ds(0, n - 1)], send_sem.at[0]).wait()
    drain(qbuf.at[pl.ds(0, n - 1)], send_sem.at[2])
    drain(kvbuf.at[pl.ds(0, n - 1)], send_sem.at[3])
    drain(obuf.at[pl.ds(0, n - 1)], send_sem.at[4])
    drain(sbuf.at[pl.ds(0, n - 1)], send_sem.at[5])

    @pl.when(seg < n_seg - 1)
    def _():
        drain(abuf, send_sem.at[1])

    drain(d1buf.at[pl.ds(0, n - 1)], recv_sem.at[7])

    @pl.when(seg > 0)
    def _():
        drain(d0buf, recv_sem.at[6])

    sums = []
    for buf in (d0buf, d1buf):
        terms = [buf[z].astype(F32) for z in range(n)]
        while len(terms) > 1:
            terms = [a + b for a, b in zip(terms[::2], terms[1::2])]
        sums.append(terms[0].astype(BF16))
    hfin_ref[...] = unstack(abuf[me].astype(F32) + sums[0].astype(F32)).astype(BF16)
    yfin_ref[...] = unstack(sums[1].astype(F32)).astype(BF16)

    drain(d1buf.at[pl.ds(0, n - 1)], send_sem.at[7])

    @pl.when(seg < n_seg - 1)
    def _():
        drain(d0buf, send_sem.at[6])


def solution(mesh):
    n = mesh.shape["tensor"]
    n_seg = mesh.shape["segment"]

    def local(h_init, y_init, norm_gain, w_query, w_kv, w_out, cache, lengths):
        hbm = pl.BlockSpec(memory_space=pl.ANY)
        vmem = pl.BlockSpec(memory_space=pltpu.VMEM)
        smem = pl.BlockSpec(memory_space=pltpu.SMEM)
        tile = (ROWS2, HD)
        wide = (ROWS2, 2 * HD)
        return pl.pallas_call(
            functools.partial(kernel, n, n_seg),
            out_shape=(
                jax.ShapeDtypeStruct(h_init.shape, BF16),
                jax.ShapeDtypeStruct(h_init.shape, BF16),
            ),
            in_specs=[hbm] * 7 + [smem],
            out_specs=(vmem, vmem),
            scratch_shapes=[
                pltpu.VMEM(h_init.shape, BF16),
                pltpu.VMEM(y_init.shape, BF16),
                pltpu.VMEM(norm_gain.shape, BF16),
                pltpu.VMEM(w_query.shape, BF16),
                pltpu.VMEM(w_kv.shape, BF16),
                pltpu.VMEM(w_out.shape, BF16),
                pltpu.VMEM(cache.shape, BF16),
                pltpu.VMEM(tile, BF16),
                pltpu.VMEM(tile, BF16),
                pltpu.VMEM((n,) + tile, BF16),
                pltpu.VMEM((n,) + tile, BF16),
                pltpu.VMEM((n,) + wide, BF16),
                pltpu.VMEM(tile, F32),
                pltpu.VMEM(tile, F32),
                pltpu.VMEM(wide, BF16),
                pltpu.VMEM((n,) + wide, BF16),
                pltpu.VMEM((ROWS2 * 2 * KVH, HD), F32),
                pltpu.VMEM((n, 2 * KVH, HD), F32),
                pltpu.VMEM((ROWS2, KVH * 16, HD), BF16),
                pltpu.VMEM((ROWS2, KVH * 16, HD), BF16),
                pltpu.VMEM((2, ROWS2 * n, HD), F32),
                pltpu.VMEM((2, ROWS2 * n, HD), F32),
                pltpu.VMEM((n,) + wide, BF16),
                pltpu.VMEM((n,) + wide, BF16),
                pltpu.VMEM((n, 1, HD), F32),
                pltpu.VMEM((n, 1, HD), F32),
                pltpu.VMEM((n,) + tile, BF16),
                pltpu.VMEM((n,) + tile, BF16),
                pltpu.VMEM((n,) + tile, BF16),
                pltpu.VMEM((n,) + tile, BF16),
                pltpu.SemaphoreType.DMA((7,)),
                pltpu.SemaphoreType.DMA((8,)),
                pltpu.SemaphoreType.DMA((8,)),
            ],
            compiler_params=pltpu.CompilerParams(
                collective_id=0, has_side_effects=True, vmem_limit_bytes=48 << 20
            ),
        )(h_init, y_init, norm_gain, w_query, w_kv, w_out, cache, lengths)

    return jax.shard_map(
        local,
        mesh=mesh,
        in_specs=(
            P("segment", "tensor"),
            P("segment", "tensor"),
            P("segment", None),
            P("segment", None, "tensor"),
            P("segment", "tensor", None),
            P("segment", "tensor", None),
            P("segment", None, "tensor", None),
            P(),
        ),
        out_specs=(P("segment", "tensor"), P("segment", "tensor")),
        check_vma=False,
    )
```

time: 545 us -> 68.9 us (0.13)
  blocking collectives: 281 us -> 0 us
  waiting for transfers between devices: 187 us -> 0 us
  Pallas kernels: 0 us -> 58 us
  other arithmetic: 39.2 us -> 0 us
  between operations: 14 us -> 0.66 us
  matrix products: 9.2 us -> 0 us
    all_gather x8 -> x0, blocking collectives: 226 us -> none  [the longest x4 109 us: merged(): everything = jax.tree.map(lambda part: lax.all_gather(part, axis), x)]
    psum x1 -> x0, waiting for transfers between devices: 132 us -> none  [local(): block_out = lax.psum(block_terms.astype(jnp.bfloat16), 'tensor')]
    pallas_call x0 -> x1, Pallas kernels: none -> 58 us  [local(): pl.pallas_call(functools.partial(kernel, n, n_seg), out_shape=(jax.ShapeD...]
    psum x1 -> x0, blocking collectives: 54.5 us -> none  [sum_fresh(): return lax.psum(kv_terms.astype(jnp.bfloat16), 'tensor').astype(jnp.float32)]
    all_gather x2 -> x0, waiting for transfers between devices: 50.8 us -> none  [merged(): everything = jax.tree.map(lambda part: lax.all_gather(part, axis), x)]
    add x63 -> x0, other arithmetic: 33.3 us -> none  [the longest x30 32.2 us: combine_parts(): first[2] * first_scale[..., None] + second[2] * second_scale[..., None]]
    unnamed x12 -> x17, local copies, waits for them, and re-layouts: 0.03 us -> 9.45 us
    dot_general x10 -> x0, matrix products: 9.2 us -> none  [the longest x2 4.46 us: local(): jnp.dot(normed, query_weight, preferred_element_type=jnp.float32)]
  transfers between devices with their start and end apart: 5 -> 0, of which waited for: 3 -> 0; matrix products, arithmetic and copies ran while one was open for 6% -> 0% of each run, Pallas kernels for 0% -> 0%
where the time goes in v1:
time: 68.9 us; the launch traced here: 68.1 us
  Pallas kernels  58 us (84%)
  local copies, waits for them, and re-layouts  9.45 us (14%)
    pallas_call x1, Pallas kernels, local(): pl.pallas_call(functools.partial(kernel, n, n_seg), out_shape=(jax.ShapeD...  58 us
    unnamed x17, local copies, waits for them, and re-layouts  9.45 us

profile of v1, /device:TPU:24, one launch (start us, length us, event | category | flops | bytes accessed | tf_op | source)
XLA Modules:
  0.0 68.1 jit_solution(13035451181696673252)
XLA Ops:
  0.6 1.3 %copy.10.cache_hbm = bf16[1,16,14,1024]{3,2,1,0:T(8,128)(2,1)S(1)} copy(bf16[1,16,14,1024]{3,1,2,0:T(8,128)(2,1)} %param.14) | data formatting | bytes 917504 | tf_op args[6]
  1.9 0.0 copy-start
  1.9 1.6 %copy-done = bf16[1,4096,256]{2,1,0:T(8,128)(2,1)S(1)} copy-done((bf16[1,4096,256]{2,1,0:T(8,128)(2,1)S(1)}, bf16[1,4096,256]{2,1,0:T(8,128)(2,1)}, u32[]{:S(2)}) %copy-start) | copy-done | bytes 2097176
  3.5 0.0 copy-start.1
  3.5 1.6 %copy-done.1 = bf16[1,256,4096]{2,1,0:T(8,128)(2,1)S(1)} copy-done((bf16[1,256,4096]{2,1,0:T(8,128)(2,1)S(1)}, bf16[1,256,4096]{2,1,0:T(8,128)(2,1)}, u32[]{:S(2)}) %copy-start.1) | copy-done | bytes 2097176
  5.1 0.0 copy-start.2
  5.1 1.0 %copy-done.2 = bf16[1,256,1024]{2,1,0:T(8,128)(2,1)S(1)} copy-done((bf16[1,256,1024]{2,1,0:T(8,128)(2,1)S(1)}, bf16[1,256,1024]{2,1,0:T(8,128)(2,1)}, u32[]{:S(2)}) %copy-start.2) | copy-done | bytes 524312
  6.1 0.0 copy-start.3
  6.1 0.7 %copy-done.3 = bf16[1,4096]{1,0:T(2,128)(2,1)S(1)} copy-done((bf16[1,4096]{1,0:T(2,128)(2,1)S(1)}, bf16[1,4096]{1,0:T(2,128)(2,1)}, u32[]{:S(2)}) %copy-start.3) | copy-done | bytes 8216
  6.9 0.0 copy-start.4
  6.9 0.7 %copy-done.4 = bf16[8,256]{1,0:T(8,128)(2,1)S(1)} copy-done((bf16[8,256]{1,0:T(8,128)(2,1)S(1)}, bf16[8,256]{1,0:T(8,128)(2,1)}, u32[]{:S(2)}) %copy-start.4) | copy-done | bytes 4120
  7.5 0.0 copy-start.5
  7.5 0.7 %copy-done.5 = bf16[8,256]{1,0:T(8,128)(2,1)S(1)} copy-done((bf16[8,256]{1,0:T(8,128)(2,1)S(1)}, bf16[8,256]{1,0:T(8,128)(2,1)}, u32[]{:S(2)}) %copy-start.5) | copy-done | bytes 4120
  8.2 0.0 copy-start.6
  8.2 0.7 copy-done.6
  8.9 58.0 %shard_map.95 = (bf16[8,256]{1,0:T(8,128)(2,1)S(1)}, bf16[8,256]{1,0:T(8,128)(2,1)S(1)}) custom-call(bf16[8,256]{1,0:T(8,128)(2,1)S(1)} %copy-done.4, bf16[8,256]{1,0:T(8,128)(2,1)S(1)} %copy-done.5, bf16[1,4096]{1,0:T(2,128)(2,1)S(1)} %copy-done.3, bf16[1,4096,256]{2,1,0:T(8,128)(2,1)S(1)} %copy-done, bf16[1,256,1024]{2,1,0:T(8,128)(2,1)S(1)} %copy-done.2, ...), custom_call_target="tpu_custom_call" | custom-call | tf_op jit(solution)/shard_map/pallas_call | solution.py:393
  66.9 0.6 copy.13
  67.5 0.6 copy.14
Async XLA Ops:
  1.9 1.6 %copy-start = (bf16[1,4096,256]{2,1,0:T(8,128)(2,1)S(1)}, bf16[1,4096,256]{2,1,0:T(8,128)(2,1)}, u32[]{:S(2)}) copy-start(bf16[1,4096,256]{2,1,0:T(8,128)(2,1)} %wq_hbm.1) | copy-start | bytes 6291460
  3.5 1.6 %copy-start.1 = (bf16[1,256,4096]{2,1,0:T(8,128)(2,1)S(1)}, bf16[1,256,4096]{2,1,0:T(8,128)(2,1)}, u32[]{:S(2)}) copy-start(bf16[1,256,4096]{2,1,0:T(8,128)(2,1)} %wo_hbm.1) | copy-start | bytes 6291460
  5.1 1.0 %copy-start.2 = (bf16[1,256,1024]{2,1,0:T(8,128)(2,1)S(1)}, bf16[1,256,1024]{2,1,0:T(8,128)(2,1)}, u32[]{:S(2)}) copy-start(bf16[1,256,1024]{2,1,0:T(8,128)(2,1)} %wkv_hbm.1) | copy-start | bytes 1572868
  6.1 0.7 %copy-start.3 = (bf16[1,4096]{1,0:T(2,128)(2,1)S(1)}, bf16[1,4096]{1,0:T(2,128)(2,1)}, u32[]{:S(2)}) copy-start(bf16[1,4096]{1,0:T(2,128)(2,1)} %gain_hbm.1) | copy-start | bytes 24580
  6.9 0.7 %copy-start.4 = (bf16[8,256]{1,0:T(8,128)(2,1)S(1)}, bf16[8,256]{1,0:T(8,128)(2,1)}, u32[]{:S(2)}) copy-start(bf16[8,256]{1,0:T(8,128)(2,1)} %h_hbm.1) | copy-start | bytes 12292
  7.5 0.7 %copy-start.5 = (bf16[8,256]{1,0:T(8,128)(2,1)S(1)}, bf16[8,256]{1,0:T(8,128)(2,1)}, u32[]{:S(2)}) copy-start(bf16[8,256]{1,0:T(8,128)(2,1)} %y_hbm.1) | copy-start | bytes 12292
  8.2 0.7 copy-start.6

commit v2 on v1

v2 whole, which is shorter than its diff:
```python
import functools
import math

import jax
import jax.numpy as jnp
from jax import lax
from jax.experimental import pallas as pl
from jax.experimental.pallas import tpu as pltpu
from jax.sharding import PartitionSpec as P

HEADS = 32
KVH = 4
HD = 128
TICKS = 2
MB = 8
ROWS2 = TICKS * MB
THETA = 500000.0
EPS = 1e-05
MASKED = -1e30
BIG = 1 << 30
MESH = pl.DeviceIdType.MESH
F32 = jnp.float32
BF16 = jnp.bfloat16


def far_first(i, me, n):
    d = n // 2 - (i + 1) // 2
    off = jnp.where(lax.rem(i, 2) == 1, d, n - d)
    return lax.rem(me + off, n)


def drain(ref, sem):
    pltpu.make_async_copy(ref, ref, sem).wait()


def stack_halves(v):
    return jnp.concatenate([v[:, :HD], v[:, HD:]], axis=0)


def unstack(v):
    return jnp.concatenate([v[:MB], v[MB:]], axis=1)


def kernel(
    n, n_seg, h_hbm, y_hbm, gain_hbm, wq_hbm, wkv_hbm, wo_hbm, cache_hbm, len_ref,
    hfin_ref, yfin_ref,
    h_in, y_in, gain, wq, wkv, wo, cache,
    ssrc_state, state, nbuf, cosb, sinb,
    qsrc, qbuf, kvt32, kvsrc, kvbuf, kvt, kbuf, vbuf, qt, ot,
    osrc, obuf, stsrc, stbuf, dsrc, dbuf,
    load_sem, send_sem, recv_sem,
):
    me = lax.axis_index("tensor")
    seg = lax.axis_index("segment")
    first = seg == 0
    not_last = seg < n_seg - 1
    span = cache_hbm.shape[1]
    slots = KVH * 16
    others = pl.ds(0, n - 1)

    barrier = pltpu.get_barrier_semaphore()

    def tell(i, carry):
        pl.semaphore_signal(
            barrier, 1, device_id={"tensor": far_first(i, me, n)}, device_id_type=MESH
        )
        return carry

    lax.fori_loop(0, n - 1, tell, 0)

    @pl.when(seg > 0)
    def _():
        def tell_back(i, carry):
            pl.semaphore_signal(
                barrier, 1, device_id={"segment": seg - 1, "tensor": i}, device_id_type=MESH
            )
            return carry

        lax.fori_loop(0, n, tell_back, 0)

    loads = [
        pltpu.make_async_copy(src, dst, load_sem.at[k])
        for k, (src, dst) in enumerate(
            [
                (h_hbm, h_in), (y_hbm, y_in), (gain_hbm, gain), (cache_hbm, cache),
                (wkv_hbm, wkv), (wq_hbm, wq), (wo_hbm, wo),
            ]
        )
    ]
    for load in loads:
        load.start()
    loads[0].wait()
    loads[1].wait()

    def send_peers(src_of, dst, sems):
        def step(i, carry):
            peer = far_first(i, me, n)
            pltpu.make_async_remote_copy(
                src_of(peer), dst, send_sem.at[sems], recv_sem.at[sems],
                device_id={"tensor": peer}, device_id_type=MESH,
            ).start()
            return carry

        lax.fori_loop(0, n - 1, step, 0)

    def send_next(src_of, dst, sems):
        @pl.when(not_last)
        def _():
            def step(i, carry):
                peer = far_first(i, me, n)
                pltpu.make_async_remote_copy(
                    src_of(peer), dst, send_sem.at[sems], recv_sem.at[sems],
                    device_id={"segment": seg + 1, "tensor": peer}, device_id_type=MESH,
                ).start()
                return carry

            lax.fori_loop(0, n - 1, step, 0)
            pltpu.make_async_remote_copy(
                src_of(me), dst, send_sem.at[sems], recv_sem.at[sems],
                device_id={"segment": seg + 1, "tensor": me}, device_id_type=MESH,
            ).start()

    h32 = h_in[...].astype(F32)
    a32 = (h32 + y_in[...].astype(F32)).astype(BF16).astype(F32)
    h_block = stack_halves(h32).astype(BF16)
    ssrc_state[0] = h_block
    ssrc_state[1] = stack_halves(a32).astype(BF16)
    state[0, me] = h_block

    row16 = lax.broadcasted_iota(jnp.int32, (ROWS2, HD), 0)
    lane16 = lax.broadcasted_iota(jnp.int32, (ROWS2, HD), 1)
    base1 = jnp.maximum(seg - 1, 0) * MB
    seen = [len_ref[seg * MB + b] for b in range(MB)] + [
        jnp.where(first, 0, len_ref[base1 + b]) for b in range(MB)
    ]
    seen_rows = jnp.zeros((ROWS2, HD), jnp.int32)
    for b in range(ROWS2):
        seen_rows = jnp.where(row16 == b, seen[b], seen_rows)
    half_lane = jnp.where(lane16 < HD // 2, lane16, lane16 - HD // 2)
    freqs = jnp.exp(-math.log(THETA) * (2.0 * half_lane.astype(F32) / HD))
    angles = seen_rows.astype(F32) * freqs
    sines = jnp.sin(angles)
    cosb[...] = jnp.cos(angles)
    sinb[...] = jnp.where(lane16 < HD // 2, -sines, sines)

    pl.semaphore_wait(barrier, jnp.where(not_last, 2 * n - 1, n - 1))

    send_peers(lambda peer: ssrc_state.at[0], state.at[0, me], 0)
    send_next(lambda peer: ssrc_state.at[1], state.at[1, me], 1)

    loads[3].wait()
    for p in range(16):
        for g in range(KVH):
            for part in range(2):
                if p < span:
                    col = (part * KVH + g) * HD
                    v = cache[0, p, :, col : col + HD].astype(F32)
                else:
                    v = jnp.zeros((ROWS2, HD), F32)
                kvt[part, pl.ds(g * 16 + p, ROWS2, stride=slots), :] = v
    for b in range(ROWS2):
        for part, dst in enumerate((kbuf, vbuf)):
            dst[b] = kvt[part, b * slots : (b + 1) * slots, :].astype(BF16)
    loads[2].wait()

    @pl.when(first)
    def _():
        state[1] = jnp.zeros_like(state[1])
        dbuf[0] = jnp.zeros_like(dbuf[0])

    loads[4].wait()
    loads[5].wait()
    jrow = lax.broadcasted_iota(jnp.int32, (HEADS, slots), 0)
    kcol = lax.broadcasted_iota(jnp.int32, (HEADS, slots), 1)
    same = lax.rem(jrow, 16) // 4 == kcol // 16
    slot = lax.rem(kcol, 16)
    place = jnp.where(same & (slot < span), me * span + slot, BIG)
    own_slot = same & (slot == span)
    lane32 = lax.broadcasted_iota(jnp.int32, (HEADS, HD), 1)
    krow = lax.broadcasted_iota(jnp.int32, (slots, HD), 0)
    scale = HD ** (-0.5)

    def project(t):
        chunks = []
        for z in range(n):
            v = state[t, z].astype(F32)
            chunks += [v[:MB], v[MB:]]
        squares = [c * c for c in chunks]
        while len(squares) > 1:
            squares = [a + b for a, b in zip(squares[::2], squares[1::2])]
        mean = jnp.sum(squares[0], axis=-1, keepdims=True) / (n * 2 * HD)
        inv = lax.rsqrt(mean + EPS)
        normed = []
        for k, c in enumerate(chunks):
            g = gain[0:1, k * HD : (k + 1) * HD].astype(F32)
            normed.append((c * inv * g).astype(BF16))
        for z in range(n):
            nbuf[z] = jnp.concatenate(normed[2 * z : 2 * z + 2], axis=1)
        kv = jnp.dot(nbuf[me], wkv[0], preferred_element_type=F32)
        for c in range(2 * KVH):
            kvt32[pl.ds(c, MB, stride=2 * KVH), :] = kv[:, c * HD : (c + 1) * HD]
        for o in range(4):
            kvsrc[t, o] = kvt32[o * 16 : (o + 1) * 16, :].astype(BF16)
        q32 = jnp.dot(jnp.concatenate(normed, axis=1), wq[0], preferred_element_type=F32)
        cosine = cosb[t * MB : (t + 1) * MB]
        sine = sinb[t * MB : (t + 1) * MB]
        turned = []
        for i in range(2):
            v = q32[:, i * HD : (i + 1) * HD]
            turned.append(v * cosine + pltpu.roll(v, HD // 2, 1) * sine)
        q = jnp.concatenate(turned, axis=0).astype(BF16)
        qsrc[t] = q
        qbuf[t, me] = q
        for o in range(4):
            owner = 4 * o + 2 * t

            @pl.when(me == owner)
            def _():
                kvbuf[t, owner] = kvsrc[t, o]

            @pl.when(me != owner)
            def _():
                pltpu.make_async_remote_copy(
                    kvsrc.at[t, o], kvbuf.at[t, me], send_sem.at[4 + t], recv_sem.at[4 + t],
                    device_id={"tensor": owner}, device_id_type=MESH,
                ).start()

        send_peers(lambda peer: qsrc.at[t], qbuf.at[t, me], 2 + t)

    def attend(t):
        @pl.when(lax.rem(me, 4) == 2 * t)
        def _():
            drain(kvbuf.at[t, others], recv_sem.at[4 + t])
            terms = [kvbuf[t, z].astype(F32) for z in range(n)]
            while len(terms) > 1:
                terms = [a + b for a, b in zip(terms[::2], terms[1::2])]
            fresh = terms[0]
            rolled = pltpu.roll(fresh, HD // 2, 1)
            for j in range(2):
                row = t * MB + (me // 4) * 2 + j
                at = j * 2 * KVH
                keys = (
                    fresh[at : at + KVH] * cosb[pl.ds(row, 1), :]
                    + rolled[at : at + KVH] * sinb[pl.ds(row, 1), :]
                )
                for dst, val in ((kbuf, keys), (vbuf, fresh[at + KVH : at + 2 * KVH])):
                    spread = jnp.concatenate(
                        [jnp.broadcast_to(val[g : g + 1], (16, HD)) for g in range(KVH)], axis=0
                    )
                    old = dst[row].astype(F32)
                    dst[row] = jnp.where(lax.rem(krow, 16) == span, spread, old).astype(BF16)

        drain(qbuf.at[t, others], recv_sem.at[2 + t])
        for r in range(n):
            v = qbuf[t, r].astype(F32)
            for i in range(2):
                qt[pl.ds(i * n + r, MB, stride=2 * n), :] = v[i * MB : (i + 1) * MB]
        scores = [
            lax.dot_general(
                qt[b * HEADS : (b + 1) * HEADS, :].astype(BF16),
                kbuf[t * MB + b],
                (((1,), (1,)), ((), ())),
                preferred_element_type=F32,
            )
            for b in range(MB)
        ]
        stats = jnp.zeros((HEADS, HD), F32)
        weights = []
        for b in range(MB):
            own_place = jnp.where(me == 4 * (b // 2) + 2 * t, -1, BIG)
            valid = jnp.where(own_slot, own_place, place) < seen[t * MB + b]
            s = jnp.where(valid, scores[b] * scale, MASKED)
            peak = jnp.max(s, axis=-1, keepdims=True)
            w = jnp.where(valid, jnp.exp(s - peak), 0.0)
            total = jnp.sum(w, axis=-1, keepdims=True)
            weights.append(w.astype(BF16))
            stats = jnp.where(lane32 == b, peak, stats)
            stats = jnp.where(lane32 == MB + b, total, stats)
        for b in range(MB):
            ot[b * HEADS : (b + 1) * HEADS, :] = jnp.dot(
                weights[b], vbuf[t * MB + b], preferred_element_type=F32
            )
        packed = jnp.where(lane32[:n] < 2 * MB, stats[:n], pltpu.roll(stats[n:], 2 * MB, 1))
        for r in range(n):
            stsrc[t, r] = packed[r : r + 1, :]
            osrc[t, r] = jnp.concatenate(
                [ot[pl.ds(i * n + r, MB, stride=2 * n), :] for i in range(2)], axis=0
            ).astype(BF16)
        obuf[t, me] = osrc[t, me]
        stbuf[t, me] = stsrc[t, me]
        send_peers(lambda peer: stsrc.at[t, peer], stbuf.at[t, me], 8 + t)
        send_peers(lambda peer: osrc.at[t, peer], obuf.at[t, me], 6 + t)

    def combine(t):
        drain(stbuf.at[t, others], recv_sem.at[8 + t])
        by_row = jnp.transpose(jnp.concatenate([stbuf[t, r] for r in range(n)], axis=0))
        shares = []
        for i in range(2):
            peaks = by_row[i * 16 : i * 16 + 8]
            totals = by_row[i * 16 + 8 : i * 16 + 16]
            scales = jnp.exp(peaks - jnp.max(peaks, axis=-1, keepdims=True))
            shares.append(scales / jnp.sum(scales * totals, axis=-1, keepdims=True))
        share = jnp.concatenate(shares, axis=0)
        drain(obuf.at[t, others], recv_sem.at[6 + t])
        terms = [obuf[t, r].astype(F32) * share[:, r : r + 1] for r in range(n)]
        while len(terms) > 1:
            terms = [a + b for a, b in zip(terms[::2], terms[1::2])]
        ctx = unstack(terms[0]).astype(BF16)
        out = jnp.dot(ctx, wo[0], preferred_element_type=F32)
        for c in range(n):
            dsrc[t, c] = stack_halves(out[:, c * 2 * HD : (c + 1) * 2 * HD]).astype(BF16)
        if t == 0:
            send_next(lambda peer: dsrc.at[0, peer], dbuf.at[0, me], 10)
        else:
            dbuf[1, me] = dsrc[1, me]
            send_peers(lambda peer: dsrc.at[1, peer], dbuf.at[1, me], 11)

    def total(t):
        terms = [dbuf[t, z].astype(F32) for z in range(n)]
        while len(terms) > 1:
            terms = [a + b for a, b in zip(terms[::2], terms[1::2])]
        return terms[0].astype(BF16).astype(F32)

    drain(state.at[0, others], recv_sem.at[0])
    project(0)

    @pl.when(seg > 0)
    def _():
        drain(state.at[1], recv_sem.at[1])

    project(1)
    attend(0)
    attend(1)
    loads[6].wait()
    combine(0)
    combine(1)

    drain(state.at[0, others], send_sem.at[0])
    for t in range(2):
        drain(qbuf.at[t, others], send_sem.at[2 + t])
        owned = lax.rem(me, 4) == 2 * t

        @pl.when(owned)
        def _():
            drain(kvsrc.at[t, pl.ds(0, 3)], send_sem.at[4 + t])

        @pl.when(jnp.logical_not(owned))
        def _():
            drain(kvsrc.at[t], send_sem.at[4 + t])

        drain(obuf.at[t, others], send_sem.at[6 + t])
        drain(stbuf.at[t, others], send_sem.at[8 + t])

    @pl.when(not_last)
    def _():
        drain(state.at[1], send_sem.at[1])
        drain(dbuf.at[0], send_sem.at[10])

    @pl.when(seg > 0)
    def _():
        drain(dbuf.at[0], recv_sem.at[10])

    hfin_ref[...] = unstack(state[1, me].astype(F32) + total(0)).astype(BF16)
    drain(dbuf.at[1, others], recv_sem.at[11])
    yfin_ref[...] = unstack(total(1)).astype(BF16)
    drain(dbuf.at[1, others], send_sem.at[11])


def solution(mesh):
    n = mesh.shape["tensor"]
    n_seg = mesh.shape["segment"]

    def local(h_init, y_init, norm_gain, w_query, w_kv, w_out, cache, lengths):
        hbm = pl.BlockSpec(memory_space=pltpu.HBM)
        vmem = pl.BlockSpec(memory_space=pltpu.VMEM)
        smem = pl.BlockSpec(memory_space=pltpu.SMEM)
        cache = jnp.transpose(cache, (0, 2, 1, 3))
        tile = (ROWS2, HD)
        return pl.pallas_call(
            functools.partial(kernel, n, n_seg),
            out_shape=(
                jax.ShapeDtypeStruct(h_init.shape, BF16),
                jax.ShapeDtypeStruct(h_init.shape, BF16),
            ),
            in_specs=[hbm] * 7 + [smem],
            out_specs=(vmem, vmem),
            scratch_shapes=[
                pltpu.VMEM(h_init.shape, BF16),
                pltpu.VMEM(y_init.shape, BF16),
                pltpu.VMEM(norm_gain.shape, BF16),
                pltpu.VMEM(w_query.shape, BF16),
                pltpu.VMEM(w_kv.shape, BF16),
                pltpu.VMEM(w_out.shape, BF16),
                pltpu.VMEM(cache.shape, BF16),
                pltpu.VMEM((2,) + tile, BF16),
                pltpu.VMEM((2, n) + tile, BF16),
                pltpu.VMEM((n, MB, 2 * HD), BF16),
                pltpu.VMEM(tile, F32),
                pltpu.VMEM(tile, F32),
                pltpu.VMEM((2,) + tile, BF16),
                pltpu.VMEM((2, n) + tile, BF16),
                pltpu.VMEM((MB * 2 * KVH, HD), F32),
                pltpu.VMEM((2, 4) + tile, BF16),
                pltpu.VMEM((2, n) + tile, BF16),
                pltpu.VMEM((2, ROWS2 * KVH * 16, HD), F32),
                pltpu.VMEM((ROWS2, KVH * 16, HD), BF16),
                pltpu.VMEM((ROWS2, KVH * 16, HD), BF16),
                pltpu.VMEM((MB * HEADS, HD), F32),
                pltpu.VMEM((MB * HEADS, HD), F32),
                pltpu.VMEM((2, n) + tile, BF16),
                pltpu.VMEM((2, n) + tile, BF16),
                pltpu.VMEM((2, n, 1, HD), F32),
                pltpu.VMEM((2, n, 1, HD), F32),
                pltpu.VMEM((2, n) + tile, BF16),
                pltpu.VMEM((2, n) + tile, BF16),
                pltpu.SemaphoreType.DMA((7,)),
                pltpu.SemaphoreType.DMA((12,)),
                pltpu.SemaphoreType.DMA((12,)),
            ],
            compiler_params=pltpu.CompilerParams(
                collective_id=0, has_side_effects=True, vmem_limit_bytes=60 << 20
            ),
        )(h_init, y_init, norm_gain, w_query, w_kv, w_out, cache, lengths)

    return jax.shard_map(
        local,
        mesh=mesh,
        in_specs=(
            P("segment", "tensor"),
            P("segment", "tensor"),
            P("segment", None),
            P("segment", None, "tensor"),
            P("segment", "tensor", None),
            P("segment", "tensor", None),
            P("segment", None, "tensor", None),
            P(),
        ),
        out_specs=(P("segment", "tensor"), P("segment", "tensor")),
        check_vma=False,
    )
```

time: 68.9 us -> 57.8 us (0.84)
  local copies, waits for them, and re-layouts: 9.45 us -> 2.53 us
  Pallas kernels: 58 us -> 54.4 us
    unnamed x17 -> x2, local copies, waits for them, and re-layouts: 9.45 us -> 2.53 us
    pallas_call x1, Pallas kernels: 58 us -> 54.4 us  [local(): pl.pallas_call(functools.partial(kernel, n, n_seg), out_shape=(jax.ShapeD...]
where the time goes in v2:
time: 57.8 us; the launch traced here: 57.6 us
  Pallas kernels  54.4 us (94%)
  local copies, waits for them, and re-layouts  2.53 us (4%)
  between operations  0.64 us (1%)
    pallas_call x1, Pallas kernels, local(): pl.pallas_call(functools.partial(kernel, n, n_seg), out_shape=(jax.ShapeD...  54.4 us
    unnamed x2, local copies, waits for them, and re-layouts  2.53 us

profile of v2, /device:TPU:24, one launch (start us, length us, event | category | flops | bytes accessed | tf_op | source)
XLA Modules:
  0.0 57.6 jit_solution(9793915807070647978)
XLA Ops:
  0.6 54.4 %shard_map.95 = (bf16[8,256]{1,0:T(8,128)(2,1)}, bf16[8,256]{1,0:T(8,128)(2,1)}) custom-call(bf16[8,256]{1,0:T(8,128)(2,1)} %h_hbm.1, bf16[8,256]{1,0:T(8,128)(2,1)} %y_hbm.1, bf16[1,4096]{1,0:T(2,128)(2,1)} %gain_hbm.1, bf16[1,4096,256]{2,1,0:T(8,128)(2,1)} %wq_hbm.1, bf16[1,256,1024]{2,1,0:T(8,128)(2,1)} %wkv_hbm.1, bf16[1,256,4096]{2,1,0:T(8,128)(2,1)} %wo_hbm.1, ...), custom_call_target="tpu_custom_call" | custom-call | tf_op jit(solution)/shard_map/pallas_call | solution.py:379
  55.0 1.3 %copy.12 = bf16[8,256]{1,0:T(8,128)(2,1)} copy(bf16[8,256]{1,0:T(8,128)(2,1)} %get-tuple-element.4) | data formatting | bytes 8192
  56.3 1.3 %copy.13 = bf16[8,256]{1,0:T(8,128)(2,1)} copy(bf16[8,256]{1,0:T(8,128)(2,1)} %get-tuple-element.5) | data formatting | bytes 8192

commit v3 on v2

--- a/solution.py
+++ b/solution.py
@@ -42,12 +42,12 @@
 
 
 def kernel(
-    n, n_seg, h_hbm, y_hbm, gain_hbm, wq_hbm, wkv_hbm, wo_hbm, cache_hbm, len_ref,
-    hfin_ref, yfin_ref,
-    h_in, y_in, gain, wq, wkv, wo, cache,
+    n, n_seg, h_hbm, y_hbm, gain_hbm, wq_hbm, wkv_hbm, wo_hbm, cache_hbm, len_hbm,
+    res_ref,
+    h_in, y_in, gain, wq, wkv, wo, cache, len_ref,
     ssrc_state, state, nbuf, cosb, sinb,
     qsrc, qbuf, kvt32, kvsrc, kvbuf, kvt, kbuf, vbuf, qt, ot,
-    osrc, obuf, stsrc, stbuf, dsrc, dbuf,
+    osrc, obuf, stsrc, stbuf, dsrc, dbuf, waiting,
     load_sem, send_sem, recv_sem,
 ):
     me = lax.axis_index("tensor")
@@ -70,20 +70,16 @@
 
     @pl.when(seg > 0)
     def _():
-        def tell_back(i, carry):
-            pl.semaphore_signal(
-                barrier, 1, device_id={"segment": seg - 1, "tensor": i}, device_id_type=MESH
-            )
-            return carry
-
-        lax.fori_loop(0, n, tell_back, 0)
+        pl.semaphore_signal(
+            barrier, 1, device_id={"segment": seg - 1, "tensor": me}, device_id_type=MESH
+        )
 
     loads = [
         pltpu.make_async_copy(src, dst, load_sem.at[k])
         for k, (src, dst) in enumerate(
             [
                 (h_hbm, h_in), (y_hbm, y_in), (gain_hbm, gain), (cache_hbm, cache),
-                (wkv_hbm, wkv), (wq_hbm, wq), (wo_hbm, wo),
+                (wkv_hbm, wkv), (wq_hbm, wq), (wo_hbm, wo), (len_hbm, len_ref),
             ]
         )
     ]
@@ -92,33 +88,23 @@
     loads[0].wait()
     loads[1].wait()
 
-    def send_peers(src_of, dst, sems):
+    def send_peers(*sends):
         def step(i, carry):
             peer = far_first(i, me, n)
-            pltpu.make_async_remote_copy(
-                src_of(peer), dst, send_sem.at[sems], recv_sem.at[sems],
-                device_id={"tensor": peer}, device_id_type=MESH,
-            ).start()
-            return carry
-
-        lax.fori_loop(0, n - 1, step, 0)
-
-    def send_next(src_of, dst, sems):
-        @pl.when(not_last)
-        def _():
-            def step(i, carry):
-                peer = far_first(i, me, n)
+            for src_of, dst, sems in sends:
                 pltpu.make_async_remote_copy(
                     src_of(peer), dst, send_sem.at[sems], recv_sem.at[sems],
-                    device_id={"segment": seg + 1, "tensor": peer}, device_id_type=MESH,
+                    device_id={"tensor": peer}, device_id_type=MESH,
                 ).start()
-                return carry
-
-            lax.fori_loop(0, n - 1, step, 0)
-            pltpu.make_async_remote_copy(
-                src_of(me), dst, send_sem.at[sems], recv_sem.at[sems],
-                device_id={"segment": seg + 1, "tensor": me}, device_id_type=MESH,
-            ).start()
+            return carry
+
+        lax.fori_loop(0, n - 1, step, 0)
+
+    def pass_on(src, dst, sems):
+        return pltpu.make_async_remote_copy(
+            src, dst, send_sem.at[sems], recv_sem.at[sems],
+            device_id={"segment": seg + 1, "tensor": me}, device_id_type=MESH,
+        )
 
     h32 = h_in[...].astype(F32)
     a32 = (h32 + y_in[...].astype(F32)).astype(BF16).astype(F32)
@@ -127,6 +113,21 @@
     ssrc_state[1] = stack_halves(a32).astype(BF16)
     state[0, me] = h_block
 
+    pl.semaphore_wait(barrier, jnp.where(not_last, n, n - 1))
+
+    @pl.when(not_last)
+    def _():
+        pass_on(ssrc_state.at[1], state.at[1, me], 12).start()
+
+    send_peers((lambda peer: ssrc_state.at[0], state.at[0, me], 0))
+
+    @pl.when(seg > 0)
+    def _():
+        drain(ssrc_state.at[1], recv_sem.at[12])
+        send_peers((lambda peer: state.at[1, me], state.at[1, me], 1))
+
+
+    loads[7].wait()
     row16 = lax.broadcasted_iota(jnp.int32, (ROWS2, HD), 0)
     lane16 = lax.broadcasted_iota(jnp.int32, (ROWS2, HD), 1)
     base1 = jnp.maximum(seg - 1, 0) * MB
@@ -142,12 +143,6 @@
     sines = jnp.sin(angles)
     cosb[...] = jnp.cos(angles)
     sinb[...] = jnp.where(lane16 < HD // 2, -sines, sines)
-
-    pl.semaphore_wait(barrier, jnp.where(not_last, 2 * n - 1, n - 1))
-
-    send_peers(lambda peer: ssrc_state.at[0], state.at[0, me], 0)
-    send_next(lambda peer: ssrc_state.at[1], state.at[1, me], 1)
-
     loads[3].wait()
     for p in range(16):
         for g in range(KVH):
@@ -166,7 +161,7 @@
     @pl.when(first)
     def _():
         state[1] = jnp.zeros_like(state[1])
-        dbuf[0] = jnp.zeros_like(dbuf[0])
+        waiting[1] = jnp.zeros_like(waiting[1])
 
     loads[4].wait()
     loads[5].wait()
@@ -225,7 +220,7 @@
                     device_id={"tensor": owner}, device_id_type=MESH,
                 ).start()
 
-        send_peers(lambda peer: qsrc.at[t], qbuf.at[t, me], 2 + t)
+        send_peers((lambda peer: qsrc.at[t], qbuf.at[t, me], 2 + t))
 
     def attend(t):
         @pl.when(lax.rem(me, 4) == 2 * t)
@@ -288,8 +283,10 @@
             ).astype(BF16)
         obuf[t, me] = osrc[t, me]
         stbuf[t, me] = stsrc[t, me]
-        send_peers(lambda peer: stsrc.at[t, peer], stbuf.at[t, me], 8 + t)
-        send_peers(lambda peer: osrc.at[t, peer], obuf.at[t, me], 6 + t)
+        send_peers(
+            (lambda peer: osrc.at[t, peer], obuf.at[t, me], 6 + t),
+            (lambda peer: stsrc.at[t, peer], stbuf.at[t, me], 8 + t),
+        )
 
     def combine(t):
         drain(stbuf.at[t, others], recv_sem.at[8 + t])
@@ -309,24 +306,22 @@
         out = jnp.dot(ctx, wo[0], preferred_element_type=F32)
         for c in range(n):
             dsrc[t, c] = stack_halves(out[:, c * 2 * HD : (c + 1) * 2 * HD]).astype(BF16)
-        if t == 0:
-            send_next(lambda peer: dsrc.at[0, peer], dbuf.at[0, me], 10)
-        else:
-            dbuf[1, me] = dsrc[1, me]
-            send_peers(lambda peer: dsrc.at[1, peer], dbuf.at[1, me], 11)
+        dbuf[t, me] = dsrc[t, me]
+        send_peers((lambda peer: dsrc.at[t, peer], dbuf.at[t, me], 10 + t))
 
     def total(t):
+        drain(dbuf.at[t, others], recv_sem.at[10 + t])
         terms = [dbuf[t, z].astype(F32) for z in range(n)]
         while len(terms) > 1:
             terms = [a + b for a, b in zip(terms[::2], terms[1::2])]
-        return terms[0].astype(BF16).astype(F32)
+        return terms[0].astype(BF16)
 
     drain(state.at[0, others], recv_sem.at[0])
     project(0)
 
     @pl.when(seg > 0)
     def _():
-        drain(state.at[1], recv_sem.at[1])
+        drain(state.at[1, others], recv_sem.at[1])
 
     project(1)
     attend(0)
@@ -335,6 +330,12 @@
     combine(0)
     combine(1)
 
+    waiting[0] = total(0)
+
+    @pl.when(not_last)
+    def _():
+        pass_on(waiting.at[0], waiting.at[1], 13).start()
+
     drain(state.at[0, others], send_sem.at[0])
     for t in range(2):
         drain(qbuf.at[t, others], send_sem.at[2 + t])
@@ -350,20 +351,25 @@
 
         drain(obuf.at[t, others], send_sem.at[6 + t])
         drain(stbuf.at[t, others], send_sem.at[8 + t])
+    drain(dbuf.at[0, others], send_sem.at[10])
+
+    @pl.when(seg > 0)
+    def _():
+        drain(state.at[1, others], send_sem.at[1])
+
+    res_ref[1] = unstack(total(1).astype(F32)).astype(BF16)
+
+    @pl.when(seg > 0)
+    def _():
+        drain(waiting.at[1], recv_sem.at[13])
+
+    res_ref[0] = unstack(state[1, me].astype(F32) + waiting[1].astype(F32)).astype(BF16)
+    drain(dbuf.at[1, others], send_sem.at[11])
 
     @pl.when(not_last)
     def _():
-        drain(state.at[1], send_sem.at[1])
-        drain(dbuf.at[0], send_sem.at[10])
-
-    @pl.when(seg > 0)
-    def _():
-        drain(dbuf.at[0], recv_sem.at[10])
-
-    hfin_ref[...] = unstack(state[1, me].astype(F32) + total(0)).astype(BF16)
-    drain(dbuf.at[1, others], recv_sem.at[11])
-    yfin_ref[...] = unstack(total(1)).astype(BF16)
-    drain(dbuf.at[1, others], send_sem.at[11])
+        drain(ssrc_state.at[1], send_sem.at[12])
+        drain(waiting.at[0], send_sem.at[13])
 
 
 def solution(mesh):
@@ -373,17 +379,13 @@
     def local(h_init, y_init, norm_gain, w_query, w_kv, w_out, cache, lengths):
         hbm = pl.BlockSpec(memory_space=pltpu.HBM)
         vmem = pl.BlockSpec(memory_space=pltpu.VMEM)
-        smem = pl.BlockSpec(memory_space=pltpu.SMEM)
         cache = jnp.transpose(cache, (0, 2, 1, 3))
         tile = (ROWS2, HD)
-        return pl.pallas_call(
+        both = pl.pallas_call(
             functools.partial(kernel, n, n_seg),
-            out_shape=(
-                jax.ShapeDtypeStruct(h_init.shape, BF16),
-                jax.ShapeDtypeStruct(h_init.shape, BF16),
-            ),
-            in_specs=[hbm] * 7 + [smem],
-            out_specs=(vmem, vmem),
+            out_shape=jax.ShapeDtypeStruct((2,) + h_init.shape, BF16),
+            in_specs=[hbm] * 8,
+            out_specs=vmem,
             scratch_shapes=[
                 pltpu.VMEM(h_init.shape, BF16),
                 pltpu.VMEM(y_init.shape, BF16),
@@ -392,6 +394,7 @@
                 pltpu.VMEM(w_kv.shape, BF16),
                 pltpu.VMEM(w_out.shape, BF16),
                 pltpu.VMEM(cache.shape, BF16),
+                pltpu.SMEM(lengths.shape, jnp.int32),
                 pltpu.VMEM((2,) + tile, BF16),
                 pltpu.VMEM((2, n) + tile, BF16),
                 pltpu.VMEM((n, MB, 2 * HD), BF16),
@@ -413,14 +416,16 @@
                 pltpu.VMEM((2, n, 1, HD), F32),
                 pltpu.VMEM((2, n) + tile, BF16),
                 pltpu.VMEM((2, n) + tile, BF16),
-                pltpu.SemaphoreType.DMA((7,)),
-                pltpu.SemaphoreType.DMA((12,)),
-                pltpu.SemaphoreType.DMA((12,)),
+                pltpu.VMEM((2,) + tile, BF16),
+                pltpu.SemaphoreType.DMA((8,)),
+                pltpu.SemaphoreType.DMA((14,)),
+                pltpu.SemaphoreType.DMA((14,)),
             ],
             compiler_params=pltpu.CompilerParams(
                 collective_id=0, has_side_effects=True, vmem_limit_bytes=60 << 20
             ),
         )(h_init, y_init, norm_gain, w_query, w_kv, w_out, cache, lengths)
+        return both[0], both[1]
 
     return jax.shard_map(
         local,

time: 57.8 us -> 52.3 us (0.905)
  Pallas kernels: 54.4 us -> 50.1 us
  local copies, waits for them, and re-layouts: 2.53 us -> 1.28 us
    pallas_call x1, Pallas kernels: 54.4 us -> 50.1 us  [local(): pl.pallas_call(functools.partial(kernel, n, n_seg), out_shape=jax.ShapeDt...]
    unnamed x2 -> x0, local copies, waits for them, and re-layouts: 2.53 us -> none
    squeeze x0 -> x1, local copies, waits for them, and re-layouts: none -> 1.28 us  [local(): return (both[0], both[1])]
where the time goes in v3:
time: 52.3 us; the launch traced here: 52 us
  Pallas kernels  50.1 us (96%)
  local copies, waits for them, and re-layouts  1.28 us (2%)
  between operations  0.64 us (1%)
    pallas_call x1, Pallas kernels, local(): pl.pallas_call(functools.partial(kernel, n, n_seg), out_shape=jax.ShapeDt...  50.1 us
    squeeze x1, local copies, waits for them, and re-layouts, local(): return (both[0], both[1])  1.28 us

profile of v3, /device:TPU:24, one launch (start us, length us, event | category | flops | bytes accessed | tf_op | source)
XLA Modules:
  0.0 52.0 jit_solution(5990080846175720400)
XLA Ops:
  0.6 50.1 %shard_map.95 = bf16[2,8,256]{2,1,0:T(8,128)(2,1)} custom-call(bf16[8,256]{1,0:T(8,128)(2,1)} %h_hbm.1, bf16[8,256]{1,0:T(8,128)(2,1)} %y_hbm.1, bf16[1,4096]{1,0:T(2,128)(2,1)} %gain_hbm.1, bf16[1,4096,256]{2,1,0:T(8,128)(2,1)} %wq_hbm.1, bf16[1,256,1024]{2,1,0:T(8,128)(2,1)} %wkv_hbm.1, bf16[1,256,4096]{2,1,0:T(8,128)(2,1)} %wo_hbm.1, ...), custom_call_target="tpu_custom_call" | custom-call | tf_op jit(solution)/shard_map/pallas_call | solution.py:384
  50.7 1.3 %slice_bitcast_fusion = (bf16[8,256]{1,0:T(8,128)(2,1)}, bf16[8,256]{1,0:T(8,128)(2,1)}) fusion(bf16[2,8,256]{2,1,0:T(8,128)(2,1)} %shard_map.95), kind=kLoop, calls=%fused_computation | loop fusion | bytes 16384 | tf_op jit(solution)/shard_map/squeeze | solution.py:428

commit v4 on v3

--- a/solution.py
+++ b/solution.py
@@ -58,15 +58,16 @@
     slots = KVH * 16
     others = pl.ds(0, n - 1)
 
+    reach = n // 4
+    near = [sign * d for d in range(reach, 0, -1) for sign in (1, -1)]
+
+    def at(off):
+        return lax.rem(me + (off + n), n)
+
     barrier = pltpu.get_barrier_semaphore()
 
-    def tell(i, carry):
-        pl.semaphore_signal(
-            barrier, 1, device_id={"tensor": far_first(i, me, n)}, device_id_type=MESH
-        )
-        return carry
-
-    lax.fori_loop(0, n - 1, tell, 0)
+    for off in near:
+        pl.semaphore_signal(barrier, 1, device_id={"tensor": at(off)}, device_id_type=MESH)
 
     @pl.when(seg > 0)
     def _():
@@ -113,19 +114,35 @@
     ssrc_state[1] = stack_halves(a32).astype(BF16)
     state[0, me] = h_block
 
-    pl.semaphore_wait(barrier, jnp.where(not_last, n, n - 1))
+    pl.semaphore_wait(barrier, jnp.where(not_last, 2 * reach + 1, 2 * reach))
 
     @pl.when(not_last)
     def _():
         pass_on(ssrc_state.at[1], state.at[1, me], 12).start()
 
-    send_peers((lambda peer: ssrc_state.at[0], state.at[0, me], 0))
-
-    @pl.when(seg > 0)
-    def _():
-        drain(ssrc_state.at[1], recv_sem.at[12])
-        send_peers((lambda peer: state.at[1, me], state.at[1, me], 1))
-
+    def spread(t, src):
+        for off in near:
+            sem = 14 + t if off == reach else 16 + t if off == -reach else t
+            pltpu.make_async_remote_copy(
+                src, state.at[t, me], send_sem.at[t], recv_sem.at[sem],
+                device_id={"tensor": at(off)}, device_id_type=MESH,
+            ).start()
+
+    def relay(t):
+        for sign, sem in ((1, 14 + t), (-1, 16 + t)):
+            block = state.at[t, at(-sign * reach)]
+            drain(block, recv_sem.at[sem])
+            for d in range(reach if sign == 1 else reach - 1, 0, -1):
+                pltpu.make_async_remote_copy(
+                    block, block, send_sem.at[t], recv_sem.at[18 + t],
+                    device_id={"tensor": at(sign * d)}, device_id_type=MESH,
+                ).start()
+
+    def gathered(t):
+        drain(state.at[t, pl.ds(0, 2 * reach - 2)], recv_sem.at[t])
+        drain(state.at[t, pl.ds(0, 2 * reach - 1)], recv_sem.at[18 + t])
+
+    spread(0, ssrc_state.at[0])
 
     loads[7].wait()
     row16 = lax.broadcasted_iota(jnp.int32, (ROWS2, HD), 0)
@@ -143,19 +160,17 @@
     sines = jnp.sin(angles)
     cosb[...] = jnp.cos(angles)
     sinb[...] = jnp.where(lane16 < HD // 2, -sines, sines)
-    loads[3].wait()
-    for p in range(16):
-        for g in range(KVH):
-            for part in range(2):
-                if p < span:
-                    col = (part * KVH + g) * HD
-                    v = cache[0, p, :, col : col + HD].astype(F32)
-                else:
-                    v = jnp.zeros((ROWS2, HD), F32)
-                kvt[part, pl.ds(g * 16 + p, ROWS2, stride=slots), :] = v
-    for b in range(ROWS2):
-        for part, dst in enumerate((kbuf, vbuf)):
-            dst[b] = kvt[part, b * slots : (b + 1) * slots, :].astype(BF16)
+    @pl.when(seg > 0)
+    def _():
+        drain(ssrc_state.at[1], recv_sem.at[12])
+        spread(1, state.at[1, me])
+
+    relay(0)
+
+    @pl.when(seg > 0)
+    def _():
+        relay(1)
+
     loads[2].wait()
 
     @pl.when(first)
@@ -316,14 +331,29 @@
             terms = [a + b for a, b in zip(terms[::2], terms[1::2])]
         return terms[0].astype(BF16)
 
-    drain(state.at[0, others], recv_sem.at[0])
+    gathered(0)
     project(0)
 
     @pl.when(seg > 0)
     def _():
-        drain(state.at[1, others], recv_sem.at[1])
+        gathered(1)
 
     project(1)
+
+    loads[3].wait()
+    for p in range(16):
+        for g in range(KVH):
+            for part in range(2):
+                if p < span:
+                    col = (part * KVH + g) * HD
+                    v = cache[0, p, :, col : col + HD].astype(F32)
+                else:
+                    v = jnp.zeros((ROWS2, HD), F32)
+                kvt[part, pl.ds(g * 16 + p, ROWS2, stride=slots), :] = v
+    for b in range(ROWS2):
+        for part, dst in enumerate((kbuf, vbuf)):
+            dst[b] = kvt[part, b * slots : (b + 1) * slots, :].astype(BF16)
+
     attend(0)
     attend(1)
     loads[6].wait()
@@ -418,8 +448,8 @@
                 pltpu.VMEM((2, n) + tile, BF16),
                 pltpu.VMEM((2,) + tile, BF16),
                 pltpu.SemaphoreType.DMA((8,)),
-                pltpu.SemaphoreType.DMA((14,)),
-                pltpu.SemaphoreType.DMA((14,)),
+                pltpu.SemaphoreType.DMA((20,)),
+                pltpu.SemaphoreType.DMA((20,)),
             ],
             compiler_params=pltpu.CompilerParams(
                 collective_id=0, has_side_effects=True, vmem_limit_bytes=60 << 20

time: 52.3 us -> 51 us (0.975)
  Pallas kernels: 50.1 us -> 48.9 us
    pallas_call x1, Pallas kernels: 50.1 us -> 48.9 us  [local(): pl.pallas_call(functools.partial(kernel, n, n_seg), out_shape=jax.ShapeDt...]
where the time goes in v4:
time: 51 us; the launch traced here: 50.9 us
  Pallas kernels  48.9 us (96%)
  local copies, waits for them, and re-layouts  1.28 us (3%)
  between operations  0.64 us (1%)
    pallas_call x1, Pallas kernels, local(): pl.pallas_call(functools.partial(kernel, n, n_seg), out_shape=jax.ShapeDt...  48.9 us
    squeeze x1, local copies, waits for them, and re-layouts, local(): return (both[0], both[1])  1.28 us

profile of v4, /device:TPU:24, one launch (start us, length us, event | category | flops | bytes accessed | tf_op | source)
XLA Modules:
  0.0 50.9 jit_solution(11591161636392465053)
XLA Ops:
  0.6 48.9 %shard_map.95 = bf16[2,8,256]{2,1,0:T(8,128)(2,1)} custom-call(bf16[8,256]{1,0:T(8,128)(2,1)} %h_hbm.1, bf16[8,256]{1,0:T(8,128)(2,1)} %y_hbm.1, bf16[1,4096]{1,0:T(2,128)(2,1)} %gain_hbm.1, bf16[1,4096,256]{2,1,0:T(8,128)(2,1)} %wq_hbm.1, bf16[1,256,1024]{2,1,0:T(8,128)(2,1)} %wkv_hbm.1, bf16[1,256,4096]{2,1,0:T(8,128)(2,1)} %wo_hbm.1, ...), custom_call_target="tpu_custom_call" | custom-call | tf_op jit(solution)/shard_map/pallas_call | solution.py:414
  49.6 1.3 %slice_bitcast_fusion = (bf16[8,256]{1,0:T(8,128)(2,1)}, bf16[8,256]{1,0:T(8,128)(2,1)}) fusion(bf16[2,8,256]{2,1,0:T(8,128)(2,1)} %shard_map.95), kind=kLoop, calls=%fused_computation | loop fusion | bytes 16384 | tf_op jit(solution)/shard_map/squeeze | solution.py:458

commit v5 on v4

--- a/solution.py
+++ b/solution.py
@@ -64,17 +64,6 @@
     def at(off):
         return lax.rem(me + (off + n), n)
 
-    barrier = pltpu.get_barrier_semaphore()
-
-    for off in near:
-        pl.semaphore_signal(barrier, 1, device_id={"tensor": at(off)}, device_id_type=MESH)
-
-    @pl.when(seg > 0)
-    def _():
-        pl.semaphore_signal(
-            barrier, 1, device_id={"segment": seg - 1, "tensor": me}, device_id_type=MESH
-        )
-
     loads = [
         pltpu.make_async_copy(src, dst, load_sem.at[k])
         for k, (src, dst) in enumerate(
@@ -84,7 +73,21 @@
             ]
         )
     ]
-    for load in loads:
+    loads[0].start()
+    loads[1].start()
+
+    barrier = pltpu.get_barrier_semaphore()
+
+    for off in near:
+        pl.semaphore_signal(barrier, 1, device_id={"tensor": at(off)}, device_id_type=MESH)
+
+    @pl.when(seg > 0)
+    def _():
+        pl.semaphore_signal(
+            barrier, 1, device_id={"segment": seg - 1, "tensor": me}, device_id_type=MESH
+        )
+
+    for load in loads[2:]:
         load.start()
     loads[0].wait()
     loads[1].wait()
@@ -99,7 +102,7 @@
                 ).start()
             return carry
 
-        lax.fori_loop(0, n - 1, step, 0)
+        lax.fori_loop(0, n - 1, step, 0, unroll=True)
 
     def pass_on(src, dst, sems):
         return pltpu.make_async_remote_copy(
@@ -322,7 +325,17 @@
         for c in range(n):
             dsrc[t, c] = stack_halves(out[:, c * 2 * HD : (c + 1) * 2 * HD]).astype(BF16)
         dbuf[t, me] = dsrc[t, me]
-        send_peers((lambda peer: dsrc.at[t, peer], dbuf.at[t, me], 10 + t))
+        def step(peer, carry):
+            @pl.when(peer != me)
+            def _():
+                pltpu.make_async_remote_copy(
+                    dsrc.at[t, peer], dbuf.at[t, me], send_sem.at[10 + t], recv_sem.at[10 + t],
+                    device_id={"tensor": peer}, device_id_type=MESH,
+                ).start()
+
+            return carry
+
+        lax.fori_loop(0, n, step, 0)
 
     def total(t):
         drain(dbuf.at[t, others], recv_sem.at[10 + t])

time: 51 us -> 50.8 us (level)
  no operation moved by 1% of the time
where the time goes in v5:
time: 50.8 us; the launch traced here: 50.5 us
  Pallas kernels  48.6 us (96%)
  local copies, waits for them, and re-layouts  1.28 us (3%)
  between operations  0.64 us (1%)
    pallas_call x1, Pallas kernels, local(): pl.pallas_call(functools.partial(kernel, n, n_seg), out_shape=jax.ShapeDt...  48.6 us
    squeeze x1, local copies, waits for them, and re-layouts, local(): return (both[0], both[1])  1.28 us

profile of v5, /device:TPU:24, one launch (start us, length us, event | category | flops | bytes accessed | tf_op | source)
XLA Modules:
  0.0 50.5 jit_solution(6369413630120016157)
XLA Ops:
  0.6 48.6 %shard_map.95 = bf16[2,8,256]{2,1,0:T(8,128)(2,1)} custom-call(bf16[8,256]{1,0:T(8,128)(2,1)} %h_hbm.1, bf16[8,256]{1,0:T(8,128)(2,1)} %y_hbm.1, bf16[1,4096]{1,0:T(2,128)(2,1)} %gain_hbm.1, bf16[1,4096,256]{2,1,0:T(8,128)(2,1)} %wq_hbm.1, bf16[1,256,1024]{2,1,0:T(8,128)(2,1)} %wkv_hbm.1, bf16[1,256,4096]{2,1,0:T(8,128)(2,1)} %wo_hbm.1, ...), custom_call_target="tpu_custom_call" | custom-call | tf_op jit(solution)/shard_map/pallas_call | solution.py:427
  49.3 1.3 %slice_bitcast_fusion = (bf16[8,256]{1,0:T(8,128)(2,1)}, bf16[8,256]{1,0:T(8,128)(2,1)}) fusion(bf16[2,8,256]{2,1,0:T(8,128)(2,1)} %shard_map.95), kind=kLoop, calls=%fused_computation | loop fusion | bytes 16384 | tf_op jit(solution)/shard_map/squeeze | solution.py:471

commit v6 on v5

--- a/solution.py
+++ b/solution.py
@@ -302,8 +302,8 @@
         obuf[t, me] = osrc[t, me]
         stbuf[t, me] = stsrc[t, me]
         send_peers(
+            (lambda peer: stsrc.at[t, peer], stbuf.at[t, me], 8 + t),
             (lambda peer: osrc.at[t, peer], obuf.at[t, me], 6 + t),
-            (lambda peer: stsrc.at[t, peer], stbuf.at[t, me], 8 + t),
         )
 
     def combine(t):

time: 50.8 us -> 50.8 us (level)
  no operation moved by 1% of the time
where the time goes in v6:
time: 50.8 us; the launch traced here: 50.4 us
  Pallas kernels  48.5 us (95%)
  local copies, waits for them, and re-layouts  1.28 us (3%)
  between operations  0.64 us (1%)
    pallas_call x1, Pallas kernels, local(): pl.pallas_call(functools.partial(kernel, n, n_seg), out_shape=jax.ShapeDt...  48.5 us
    squeeze x1, local copies, waits for them, and re-layouts, local(): return (both[0], both[1])  1.28 us

profile of v6, /device:TPU:24, one launch (start us, length us, event | category | flops | bytes accessed | tf_op | source)
XLA Modules:
  0.0 50.4 jit_solution(8426423146543681429)
XLA Ops:
  0.6 48.5 %shard_map.95 = bf16[2,8,256]{2,1,0:T(8,128)(2,1)} custom-call(bf16[8,256]{1,0:T(8,128)(2,1)} %h_hbm.1, bf16[8,256]{1,0:T(8,128)(2,1)} %y_hbm.1, bf16[1,4096]{1,0:T(2,128)(2,1)} %gain_hbm.1, bf16[1,4096,256]{2,1,0:T(8,128)(2,1)} %wq_hbm.1, bf16[1,256,1024]{2,1,0:T(8,128)(2,1)} %wkv_hbm.1, bf16[1,256,4096]{2,1,0:T(8,128)(2,1)} %wo_hbm.1, ...), custom_call_target="tpu_custom_call" | custom-call | tf_op jit(solution)/shard_map/pallas_call | solution.py:427
  49.1 1.3 %slice_bitcast_fusion = (bf16[8,256]{1,0:T(8,128)(2,1)}, bf16[8,256]{1,0:T(8,128)(2,1)}) fusion(bf16[2,8,256]{2,1,0:T(8,128)(2,1)} %shard_map.95), kind=kLoop, calls=%fused_computation | loop fusion | bytes 16384 | tf_op jit(solution)/shard_map/squeeze | solution.py:471

commit v7 on v5

--- a/solution.py
+++ b/solution.py
@@ -224,7 +224,8 @@
         q = jnp.concatenate(turned, axis=0).astype(BF16)
         qsrc[t] = q
         qbuf[t, me] = q
-        for o in range(4):
+        for k in (2, 1, 3, 0):
+            o = lax.rem(me // 4 + k, 4)
             owner = 4 * o + 2 * t
 
             @pl.when(me == owner)

time: 50.8 us -> 51 us (level)
  no operation moved by 1% of the time
where the time goes in v7:
time: 51 us; the launch traced here: 50.7 us
  Pallas kernels  48.7 us (95%)
  local copies, waits for them, and re-layouts  1.28 us (3%)
  between operations  0.64 us (1%)
    pallas_call x1, Pallas kernels, local(): pl.pallas_call(functools.partial(kernel, n, n_seg), out_shape=jax.ShapeDt...  48.7 us
    squeeze x1, local copies, waits for them, and re-layouts, local(): return (both[0], both[1])  1.28 us

profile of v7, /device:TPU:24, one launch (start us, length us, event | category | flops | bytes accessed | tf_op | source)
XLA Modules:
  0.0 50.7 jit_solution(14927440213859364480)
XLA Ops:
  0.6 48.7 %shard_map.95 = bf16[2,8,256]{2,1,0:T(8,128)(2,1)} custom-call(bf16[8,256]{1,0:T(8,128)(2,1)} %h_hbm.1, bf16[8,256]{1,0:T(8,128)(2,1)} %y_hbm.1, bf16[1,4096]{1,0:T(2,128)(2,1)} %gain_hbm.1, bf16[1,4096,256]{2,1,0:T(8,128)(2,1)} %wq_hbm.1, bf16[1,256,1024]{2,1,0:T(8,128)(2,1)} %wkv_hbm.1, bf16[1,256,4096]{2,1,0:T(8,128)(2,1)} %wo_hbm.1, ...), custom_call_target="tpu_custom_call" | custom-call | tf_op jit(solution)/shard_map/pallas_call | solution.py:428
  49.4 1.3 %slice_bitcast_fusion = (bf16[8,256]{1,0:T(8,128)(2,1)}, bf16[8,256]{1,0:T(8,128)(2,1)}) fusion(bf16[2,8,256]{2,1,0:T(8,128)(2,1)} %shard_map.95), kind=kLoop, calls=%fused_computation | loop fusion | bytes 16384 | tf_op jit(solution)/shard_map/squeeze | solution.py:472
